TPU v7x, 256 devices: a whole 4x4x8 slice. The times are simulated.
256 devices in a mesh: row: 16 (over y, x_lo, core), col: 16 (over z, x_hi).
Axes of the slice: x: 4 (x_hi: 2, x_lo: 2; x = x_hi * 2 + x_lo), y: 4, z: 8, core: 2. Of those that a mesh axis runs over, the one named last changes fastest.
Arguments:
- features: bfloat16 [32768, 1024], P(('row', 'col')), may hold values from -6 to 6
- node_valid: int32 [256, 128], P(('row', 'col')), may hold values 0 or 1
- self_mask: int32 [256, 128, 128], P(('row', 'col')), may hold values 0 or 1
- pair_blocks: int32 [16, 16, 8, 2], P('row', 'col'), may hold values from 0 to 255, as said below
- pair_count: int32 [16, 16], P('row', 'col'), may hold values from 0 to 8, as said below
- pair_masks: int32 [16, 16, 8, 128, 128], P('row', 'col'), may hold values 0 or 1
- weight_src: bfloat16 [1024, 1024], replicated, may hold values from -0.1875 to 0.1875
- weight_tgt: bfloat16 [1024, 1024], replicated, may hold values from -0.1875 to 0.1875
- attn: float32 [4, 256], replicated
- bias: float32 [1024], replicated, may hold values from -6 to 6
Outputs:
- attended: bfloat16 [32768, 1024], P(('row', 'col'))
Inputs may be any that keep to these rules, and one draw needn't show every extreme that they name: `pair_blocks`: cell (r, c) lists in each slot a pair (i, j) of different blocks: i is held by a device of grid row r and j by a device of grid column c, block b being held by device b // 1 counted row by row. No unordered pair stands in two live slots. Slots from pair_count on are not used. Some cell has all 8 slots live.
All inputs are finite; a program needn't handle non-finite values. No bound on the sum of `node_valid` or of `self_mask` or of `pair_masks` on one device may be relied on, other than what follows from the above.
Results may differ from a plain program's by a relative error of at most 0.012.
The roundings to bfloat16 on the way count: a program that leaves them out, or rounds other values in their place, can miss the bound.
Values may be sent and summed in bfloat16 or wider, within the bound.
No kernel may reach another device: no remote copies, remote signals or barrier semaphores. Data moves between devices by JAX's collectives and lax.ppermute only.
A program may use at most 128 MiB of HBM per device.

v0:
```python
import functools

import jax
import jax.numpy as jnp
from jax import lax
from jax.experimental import pallas as pl
from jax.experimental.pallas import tpu as pltpu
from jax.sharding import Mesh, PartitionSpec as P

F32 = jnp.float32
BF16 = jnp.bfloat16
FLOOR = -1e30
BS = 128
HS = 256
EXT = 16
SRC = BS + EXT
ALL = SRC + BS
PER_DOT = 4


def split3(value):
    high = value.astype(BF16).astype(F32)
    rest = value - high
    middle = rest.astype(BF16).astype(F32)
    return high, middle, rest - middle


def pack_rows(value):
    high, middle, low = split3(jnp.broadcast_to(value, (EXT, BS)))
    row = lax.broadcasted_iota(jnp.int32, (EXT, BS), 0)
    zero = jnp.zeros_like(high)
    rows = jnp.where(row == 0, high, jnp.where(row == 1, middle, jnp.where(row == 2, low, zero)))
    return jnp.concatenate([rows, zero], axis=1).astype(BF16)


def unpack_rows(rows):
    wide = rows.astype(F32)
    return wide[0:1] + (wide[1:2] + wide[2:3])


def project_kernel(place, features, valid, attn, weight_src, weight_tgt, *outs):
    step = pl.program_id(0)
    source = jnp.dot(features[...], weight_src[...], preferred_element_type=F32).astype(BF16)
    target = jnp.dot(features[...], weight_tgt[...], preferred_element_type=F32).astype(BF16)
    linear = jnp.sum(
        source.astype(F32) * attn[pl.ds(step ^ place[0], 1), :], axis=1, keepdims=True
    )
    linear = jnp.broadcast_to(linear, (BS, BS)).T[0:1]
    extra = pack_rows(jnp.where(valid[...] > 0, linear, FLOOR))
    for d, out in enumerate(outs):

        @pl.when(step == d)
        def _():
            out[:BS, :] = source
            out[BS:SRC, :] = extra
            out[SRC:, :] = target


def project(place, features, valid, attn, weight_src, weight_tgt):
    heads = attn.shape[0]
    width = features.shape[1]
    return pl.pallas_call(
        project_kernel,
        grid_spec=pltpu.PrefetchScalarGridSpec(
            num_scalar_prefetch=1,
            grid=(heads,),
            in_specs=[
                pl.BlockSpec((BS, width), lambda d, place: (0, 0)),
                pl.BlockSpec((1, BS), lambda d, place: (0, 0)),
                pl.BlockSpec((heads, HS), lambda d, place: (0, 0)),
                pl.BlockSpec((width, HS), lambda d, place: (0, d ^ place[0])),
                pl.BlockSpec((width, HS), lambda d, place: (0, d ^ place[0])),
            ],
            out_specs=[pl.BlockSpec((ALL, HS), lambda d, place: (0, 0))] * heads,
        ),
        out_shape=[jax.ShapeDtypeStruct((ALL, HS), BF16)] * heads,
        name="project",
    )(place, features, valid, attn, weight_src, weight_tgt)


def gather_kernel(*refs):
    parts, (source, target) = refs[:4], refs[4:]
    for d, part in enumerate(parts):
        source[d] = part[:SRC, :]
        target[d] = part[SRC:, :]


def gather_square(parts):
    return pl.pallas_call(
        gather_kernel,
        out_shape=[
            jax.ShapeDtypeStruct((4, SRC, HS), BF16),
            jax.ShapeDtypeStruct((4, BS, HS), BF16),
        ],
        name="gather_square",
    )(*parts)


def pair_kernel(first, second, out):
    out[:4] = first[...]
    out[4:] = second[...]


def pair(first, second):
    return pl.pallas_call(
        pair_kernel, out_shape=jax.ShapeDtypeStruct((8, *first.shape[1:]), BF16), name="pair"
    )(first, second)


def score_plane(target, minus, wide, halves, scaled, planes):
    lane = lax.broadcasted_iota(jnp.int32, (BS, BS), 1)
    half = BS // 2
    wide[...] = target.astype(F32)
    tiled = wide[...].astype(BF16).reshape(BS // 16, 16, HS)
    weights = halves[...]
    left, right = scaled[:, :BS], scaled[:, BS:]
    waiting = []

    def flush():
        tiles = []
        for u, side in waiting:
            row = minus[u + side * half : u + side * half + 1, :]
            row = jnp.broadcast_to(row, (16, HS)).astype(BF16)
            tiles.append(jnp.maximum(tiled, row[None]).reshape(BS, HS))
        sums = jnp.dot(jnp.concatenate(tiles), weights, preferred_element_type=F32)
        for at, (u, side) in enumerate(waiting):
            pltpu.store(
                planes.at[side], sums[at * BS : (at + 1) * BS], mask=(lane == u) | (lane == u + half)
            )
        waiting.clear()

    for u in range(half):
        for side in range(2):
            if u % 2 == 0:
                waiting.append((u, side))
                if len(waiting) == PER_DOT:
                    flush()
            else:
                s = u + side * half
                row = minus[s : s + 1, :]
                terms = (
                    jnp.maximum(wide[:, :BS], row[:, :BS]) * left
                    + jnp.maximum(wide[:, BS:], row[:, BS:]) * right
                )
                sums = jnp.broadcast_to(jnp.sum(terms, axis=1, keepdims=True), (BS, BS))
                pltpu.store(planes.at[2], sums, mask=lane == s)
    low, high = planes[0], planes[1]
    low = low + pltpu.roll(low, half, 1)
    high = high + pltpu.roll(high, half, 1)
    return jnp.where(lane % 2 == 1, planes[2], jnp.where(lane < half, low, high))


def attend_kernel(kind, split, *refs):
    if kind == "self":
        target_pieces, source_pieces, (masks, halves, scaled, out, acc, peak, den, minus, wide, planes) = refs[:1], refs[1:2], refs[2:]
        targets, sources = target_pieces[0], source_pieces[0]
    else:
        count, target_at, source_at, out_at, masks, halves, scaled = refs[:7]
        target_pieces, source_pieces = refs[7 : 7 + split[0]], refs[7 + split[0] : 7 + sum(split)]
        out, acc, peak, den, minus, wide, planes, targets, sources, sems = refs[7 + sum(split) :]
    blocks = acc.shape[0]
    copies = []
    if kind != "self":
        for pieces, table in ((target_pieces, targets), (source_pieces, sources)):
            at = 0
            for piece in pieces:
                size = piece.shape[0]
                copies.append(
                    pltpu.make_async_copy(piece, table.at[pl.ds(at, size)], sems.at[len(copies)])
                )
                at += size
    for copy in copies:
        copy.start()

    def clear(b, carry):
        acc[b] = jnp.zeros((BS, HS), F32)
        peak[b] = jnp.full((BS, BS), FLOOR, F32)
        den[b] = jnp.zeros((BS, BS), F32)
        return carry

    lax.fori_loop(0, blocks, clear, 0)
    for copy in copies:
        copy.wait()

    def one(cell, slot, a, b, c):
        source = sources[b, :BS, :]
        minus[...] = -source.astype(F32)
        linear = unpack_rows(sources[b, BS:SRC, :BS])
        scores = score_plane(targets[a], minus, wide, halves, scaled[...], planes)
        mask = masks[cell, pl.ds(pl.multiple_of(slot * BS, BS), BS), :].astype(F32)
        if kind == "backward":
            mask = mask.T
        scores = jnp.where(mask > 0, scores + linear, FLOOR)
        before = peak[c]
        top = jnp.maximum(before, jnp.max(scores, axis=1, keepdims=True))
        scale = jnp.exp(before - top)
        weights = jnp.exp(scores - top)
        peak[c] = top
        den[c] = den[c] * scale + jnp.sum(weights, axis=1, keepdims=True)
        acc[c] = acc[c] * jnp.concatenate([scale, scale], axis=1) + jnp.dot(
            weights.astype(BF16), source, preferred_element_type=F32
        )

    if kind == "self":

        def own_step(b, carry):
            one(b, 8, b, b, b)
            return carry

        lax.fori_loop(0, blocks, own_step, 0)
    else:
        ends = [count[0], count[0] + count[1], count[0] + count[1] + count[2]]

        def step(i, carry):
            cell, start = jnp.int32(0), jnp.int32(0)
            for end in ends:
                past = i >= end
                cell = cell + jnp.where(past, 1, 0)
                start = jnp.where(past, end, start)
            slot = i - start
            at = cell * 8 + slot
            one(cell, slot, target_at[at], source_at[at], out_at[at])
            return carry

        lax.fori_loop(0, ends[2] + count[3], step, 0)

    def finish(b, carry):
        total = jnp.maximum(den[b], 1e-30)
        inverse = 1.0 / total
        out[b, :BS, :] = (acc[b] * jnp.concatenate([inverse, inverse], axis=1)).astype(BF16)
        out[b, BS:, :] = pack_rows((peak[b] + jnp.log(total)).T[0:1])
        return carry

    lax.fori_loop(0, blocks, finish, 0)


def attend(kind, lists, masks, attn, targets, sources):
    smem = pl.BlockSpec(memory_space=pltpu.SMEM)
    vmem = pl.BlockSpec(memory_space=pltpu.VMEM)
    hbm = pl.BlockSpec(memory_space=pltpu.HBM)
    split = (len(targets), len(sources))
    blocks = 4 if kind == "self" else 32
    slots = 4 if kind == "self" else 16
    scratch = [
        pltpu.VMEM((blocks, BS, HS), F32),
        pltpu.VMEM((blocks, BS, BS), F32),
        pltpu.VMEM((blocks, BS, BS), F32),
        pltpu.VMEM((BS, HS), F32),
        pltpu.VMEM((BS, HS), F32),
        pltpu.VMEM((3, BS, BS), F32),
    ]
    if kind == "self":
        operands = (*targets, *sources, masks, *attn)
        specs = [vmem] * 5
    else:
        operands = (*lists, masks, *attn, *targets, *sources)
        specs = [smem] * 4 + [vmem] * 3 + [hbm] * sum(split)
        scratch += [
            pltpu.VMEM((blocks, BS, HS), BF16),
            pltpu.VMEM((blocks, SRC, HS), BF16),
            pltpu.SemaphoreType.DMA((sum(split),)),
        ]
    return pl.pallas_call(
        functools.partial(attend_kernel, kind, split),
        out_shape=jax.ShapeDtypeStruct((blocks, SRC, HS), BF16),
        in_specs=specs,
        out_specs=vmem,
        scratch_shapes=scratch,
        compiler_params=pltpu.CompilerParams(vmem_limit_bytes=(16 if kind == "self" else 56) << 20),
        cost_estimate=pl.CostEstimate(
            flops=slots * BS * BS * HS * 512, bytes_accessed=1 << 20, transcendentals=0
        ),
        name="attend_" + kind,
    )(*operands)


def merge_kernel(place, rows, cols, own, bias, out):
    parts = [rows.at[p, 0] for p in range(8)] + [cols.at[p, 0] for p in range(8)] + [own.at[0]]
    sums = [unpack_rows(part[BS:SRC, :BS]) for part in parts]
    top = functools.reduce(jnp.maximum, sums)
    shares = [jnp.exp(value - top) for value in sums]
    total = functools.reduce(jnp.add, shares)
    table = jnp.concatenate([share / total for share in shares] + [jnp.zeros((BS - 17, BS), F32)])
    table = table.T
    result = jnp.zeros((BS, HS), F32)
    for p, part in enumerate(parts):
        result = result + part[:BS, :].astype(F32) * table[:, p : p + 1]
    out[0] = (result + bias[...]).astype(BF16)


def merge(place, rows, cols, own, bias):
    blocks = own.shape[0]
    return pl.pallas_call(
        merge_kernel,
        grid_spec=pltpu.PrefetchScalarGridSpec(
            num_scalar_prefetch=1,
            grid=(blocks,),
            in_specs=[
                pl.BlockSpec((8, 1, SRC, HS), lambda d, place: (0, d, 0, 0)),
                pl.BlockSpec((8, 1, SRC, HS), lambda d, place: (0, d, 0, 0)),
                pl.BlockSpec((1, SRC, HS), lambda d, place: (d, 0, 0)),
                pl.BlockSpec((1, HS), lambda d, place: (0, 0)),
            ],
            out_specs=pl.BlockSpec((1, BS, HS), lambda d, place: (d ^ place[0], 0, 0)),
        ),
        out_shape=jax.ShapeDtypeStruct((blocks, BS, HS), BF16),
        name="merge",
    )(place, rows, cols, own, bias)


def body(
    features,
    node_valid,
    self_mask,
    pair_blocks,
    pair_count,
    pair_masks,
    weight_src,
    weight_tgt,
    attn,
    bias,
):
    heads = attn.shape[0]
    group = ("rp", "cp")
    row_part, col_part = lax.axis_index("rp"), lax.axis_index("cp")
    head = row_part * 2 + col_part

    place = head.reshape(1)

    def swap(d, value):
        return lax.ppermute(value, group, [(i, i ^ d) for i in range(4)])

    sent = project(place, features, node_valid, attn, weight_src, weight_tgt)
    sent, pair_masks = lax.optimization_barrier((sent, pair_masks))
    mine = [sent[0]] + [swap(d, sent[d]) for d in (1, 2, 3)]

    identity = jnp.eye(BS, dtype=bool)
    own_mask = (self_mask[0] > 0) | identity
    first, second = pair_blocks[0, 0, :, 0] % 16, pair_blocks[0, 0, :, 1] // 16
    first_at = (first // 2) * 4 + row_part * 2 + first % 2
    second_at = (second // 2) * 4 + (second % 2) * 2 + col_part
    info = jnp.stack([first_at, second_at, jnp.broadcast_to(pair_count[0, 0], (8,))])
    info = jnp.pad(info, ((0, EXT - 3), (0, BS - 8)))
    cell = jnp.concatenate(
        [
            pair_masks.reshape(8 * BS, BS).astype(BF16),
            own_mask.astype(BF16),
            info.astype(BF16),
        ]
    )
    cells = jnp.stack([cell] + [swap(d, cell) for d in (1, 2, 3)])
    lists = cells[:, 9 * BS : 9 * BS + 3, :8].astype(jnp.int32)
    first_at, second_at = lists[:, 0].reshape(32) ^ head, lists[:, 1].reshape(32) ^ head
    count = lists[:, 2, 0]
    me = lax.axis_index("R")
    from_row = second_at // 4
    y_steps = (me // 2 - from_row // 2) % 4
    x_steps = (me + from_row) % 2
    second_near = (y_steps * 2 + x_steps) * 4 + second_at % 4

    source, target = gather_square(mine)

    size = lax.axis_size("R")
    across = [(i, i ^ 1) for i in range(size)]
    around = [[(i, (i + 2 * k) % size) for i in range(size)] for k in (1, 2, 3)]
    row_targets = lax.all_gather(target, "C", axis=0, tiled=True)
    source_beside = lax.ppermute(source, "R", across)
    target_beside = lax.ppermute(target, "R", across)
    col_sources = [source, source_beside]
    for way in around:
        col_sources += [lax.ppermute(source, "R", way), lax.ppermute(source_beside, "R", way)]

    scaled = 0.8 * lax.dynamic_index_in_dim(attn, head, 0, keepdims=False)
    high = lax.reduce_precision(scaled, 8, 7)
    low = scaled - high
    halves = jnp.concatenate(
        [jnp.broadcast_to(part[:, None], (HS, BS // 2)) for part in (high, low)], axis=1
    ).astype(BF16)
    shared = (halves, scaled[None])

    own = attend("self", (), cells, shared, [target], [source])
    both = pair(target, target_beside)
    (row_targets, *col_sources), both, later_source, own = lax.optimization_barrier(
        ((row_targets, *col_sources), both, source, own)
    )
    row_sources = lax.all_gather(later_source, "C", axis=0, tiled=True)
    col_targets = [both] + [lax.ppermute(both, "R", way) for way in around]
    to_rows = attend(
        "forward", (count, first_at, second_near, first_at), cells, shared, [row_targets], col_sources
    )
    to_rows, col_targets = lax.optimization_barrier((to_rows, col_targets))
    to_cols = attend(
        "backward", (count, second_near, first_at, second_at), cells, shared, col_targets, [row_sources]
    )
    rows = lax.all_to_all(to_rows, "C", 0, 0, tiled=True).reshape(8, 4, SRC, HS)
    cols = lax.all_to_all(to_cols, "R", 0, 0, tiled=True).reshape(8, 4, SRC, HS)
    bias_head = lax.dynamic_index_in_dim(bias.reshape(heads, HS), head, 0)
    merged = merge(place, rows, cols, own, bias_head)
    merged = lax.all_to_all(merged, group, 0, 0, tiled=True)
    result = merged.transpose(1, 0, 2).reshape(BS, heads * HS)
    return jnp.where(node_valid[0][:, None] > 0, result, bias.astype(BF16)[None, :])


def solution(mesh):
    fine = Mesh(mesh.devices.reshape(8, 2, 8, 2), ("R", "rp", "C", "cp"))
    row, col = ("R", "rp"), ("C", "cp")
    both = row + col
    return jax.shard_map(
        body,
        mesh=fine,
        in_specs=(
            P(both, None),
            P(both, None),
            P(both, None, None),
            P(row, col, None, None),
            P(row, col),
            P(row, col, None, None, None),
            P(),
            P(),
            P(),
            P(),
        ),
        out_specs=P(both, None),
        check_vma=False,
    )
```

profile of v0, /device:TPU:64, one launch (start us, length us, event | category | flops | bytes accessed | tf_op | source)
XLA Modules:
  0.0 248.3 jit_solution(5603086784877073575)
XLA Ops:
  6.5 4.8 %project.1 = (bf16[272,256]{1,0:T(8,128)(2,1)}, bf16[272,256]{1,0:T(8,128)(2,1)}, bf16[272,256]{1,0:T(8,128)(2,1)}, bf16[272,256]{1,0:T(8,128)(2,1)}) custom-call(s32[1]{0:T(128)} %bitcast.1.place, bf16[128,1024]{1,0:T(8,128)(2,1)} %features.1, s32[1,128]{1,0:T(1,128)} %valid.1, f32[4,256]{1,0:T(4,128)} %attn.1, bf16[1024,1024]{1,0:T(8,128)(2,1)} %weight_src.1, ...), custom_call_target="tpu_custom_call" | custom-call | tf_op jit(solution)/shard_map/project/pallas_call | solution.py:62
  11.4 3.1 %collective-permute-start.3 = (bf16[272,256]{1,0:T(8,128)(2,1)}, bf16[272,256]{1,0:T(8,128)(2,1)S(1)}, u32[]{:S(2)}, u32[]{:S(2)}) collective-permute-start(bf16[272,256]{1,0:T(8,128)(2,1)} %get-tuple-element.39), channel_id=1, source_target_pairs={{0,1},{1,0},{16,17},{17,16},{2,3},{3,2},{18,19},{19,18},{4,5},{5,4... | collective-permute-start | bytes 417800 | tf_op jit(solution)/shard_map/ppermute | solution.py:331
  15.1 3.8 %collective-permute-done.3.refs_1_ = bf16[272,256]{1,0:T(8,128)(2,1)S(1)} collective-permute-done((bf16[272,256]{1,0:T(8,128)(2,1)}, bf16[272,256]{1,0:T(8,128)(2,1)S(1)}, u32[]{:S(2)}, u32[]{:S(2)}) %collective-permute-start.3) | collective-permute-done | bytes 139296 | tf_op jit(solution)/shard_map/ppermute | solution.py:331
  18.9 2.6 %collective-permute-done.5.refs_3_ = bf16[272,256]{1,0:T(8,128)(2,1)S(1)} collective-permute-done((bf16[272,256]{1,0:T(8,128)(2,1)}, bf16[272,256]{1,0:T(8,128)(2,1)S(1)}, u32[]{:S(2)}, u32[]{:S(2)}) %collective-permute-start.5) | collective-permute-done | bytes 139296 | tf_op jit(solution)/shard_map/ppermute | solution.py:331
  22.2 1.9 gather_square.1
  25.2 2.6 %collective-permute-start.2 = (bf16[1168,128]{1,0:T(8,128)(2,1)S(1)}, bf16[1168,128]{1,0:T(8,128)(2,1)S(1)}, u32[]{:S(2)}, u32[]{:S(2)}) collective-permute-start(bf16[1168,128]{1,0:T(8,128)(2,1)S(1)} %get-tuple-element.64), channel_id=1, source_target_pairs={{0,17},{1,16},{16,1},{17,0},{2,19},{3,18},{18,3},{19,2},{4,21},{5,... | collective-permute-start | bytes 897032 | tf_op jit(solution)/shard_map/ppermute | solution.py:331
  32.8 2.8 %collective-permute-done.2 = bf16[1168,128]{1,0:T(8,128)(2,1)S(1)} collective-permute-done((bf16[1168,128]{1,0:T(8,128)(2,1)S(1)}, bf16[1168,128]{1,0:T(8,128)(2,1)S(1)}, u32[]{:S(2)}, u32[]{:S(2)}) %collective-permute-start.2) | collective-permute-done | bytes 299040 | tf_op jit(solution)/shard_map/ppermute | solution.py:331
  35.6 3.2 %collective-permute-start.9 = (bf16[4,144,256]{2,1,0:T(8,128)(2,1)S(1)}, bf16[4,144,256]{2,1,0:T(8,128)(2,1)S(1)}, u32[]{:S(2)}, u32[]{:S(2)}) collective-permute-start(bf16[4,144,256]{2,1,0:T(8,128)(2,1)S(1)} %copy-done.3), channel_id=1, source_target_pairs={{0,128},{32,160},{64,192},{96,224},{128,0},{160,32},{192,64},{224,... | collective-permute-start | bytes 884744 | tf_op jit(solution)/shard_map/ppermute | solution.py:371
  39.8 3.4 %collective-permute-done = bf16[1168,128]{1,0:T(8,128)(2,1)S(1)} collective-permute-done((bf16[1168,128]{1,0:T(8,128)(2,1)S(1)}, bf16[1168,128]{1,0:T(8,128)(2,1)S(1)}, u32[]{:S(2)}, u32[]{:S(2)}) %collective-permute-start) | collective-permute-done | bytes 299040 | tf_op jit(solution)/shard_map/ppermute | solution.py:331
  44.3 6.9 %attend_self.1.own = bf16[4,144,256]{2,1,0:T(8,128)(2,1)S(1)} custom-call(bf16[4,128,256]{2,1,0:T(8,128)(2,1)S(1)} %copy-done.1, bf16[4,144,256]{2,1,0:T(8,128)(2,1)S(1)} %copy-done.3, bf16[4,1168,128]{2,1,0:T(8,128)(2,1)S(1)} %pad_maximum_fusion.refs_2_.refs_4_, bf16[256,128]{1,0:T(8,128)(2,1)S(1)} %pad_maximum_fusion.1.refs_3_.refs_5_, ...), custom_call_target="tpu_custom_call" | custom-call | flops 8589934592 | bytes 1048576 | tf_op jit(solution)/shard_map/attend_self/pallas_call | solution.py:263
  54.2 2.9 %collective-permute-start.10 = (bf16[4,144,256]{2,1,0:T(8,128)(2,1)S(1)}, bf16[4,144,256]{2,1,0:T(8,128)(2,1)S(1)}, u32[]{:S(2)}, u32[]{:S(2)}) collective-permute-start(bf16[4,144,256]{2,1,0:T(8,128)(2,1)S(1)} %collective-permute-done.6.refs_9_), channel_id=1, source_target_pairs={{0,128},{32,160},{64,192},{96,224},{128,0},{160,32},{192,64},{224,... | collective-permute-start | bytes 884744 | tf_op jit(solution)/shard_map/ppermute | solution.py:371
  59.8 1.9 pair.1.refs_7_
  62.7 7.0 %collective-permute-done.10.refs_13_ = bf16[4,144,256]{2,1,0:T(8,128)(2,1)S(1)} collective-permute-done((bf16[4,144,256]{2,1,0:T(8,128)(2,1)S(1)}, bf16[4,144,256]{2,1,0:T(8,128)(2,1)S(1)}, u32[]{:S(2)}, u32[]{:S(2)}) %collective-permute-start.10) | collective-permute-done | bytes 294944 | tf_op jit(solution)/shard_map/ppermute | solution.py:371
  70.0 1.9 collective-permute-start.14
  71.9 2.4 collective-permute-start.15
  75.2 40.0 %attend_forward.1 = bf16[32,144,256]{2,1,0:T(8,128)(2,1)} custom-call(s32[4]{0:T(128)} %slice_reduce_fusion.refs_0_, s32[32]{0:T(128)} %xor.16.refs_1_.refs_3_.refs_2_, s32[32]{0:T(128)} %fusion.9.refs_2_.refs_1_, s32[32]{0:T(128)} %xor.16.refs_1_.refs_3_.refs_2_, bf16[4,1168,128]{2,1,0:T(8,128)(2,1)} %copy-done, bf16[256,128]{1,0:T(8,128)(2,1)} %copy-done.4, ...), custom_call_target="tpu_custom_call" | custom-call | flops 34359738368 | bytes 1048576 | tf_op jit(solution)/shard_map/attend_forward/pallas_call | solution.py:263
  116.4 5.7 %all-to-all-start = ((bf16[32,144,256]{2,1,0:T(8,128)(2,1)}), bf16[32,144,256]{2,1,0:T(8,128)(2,1)S(1)}, u32[]{:S(2)}, u32[]{:S(2)}) async-start(bf16[32,144,256]{2,1,0:T(8,128)(2,1)} %attend_forward.1), calls=%async_computation | async-start | bytes 4718592 | tf_op jit(solution)/shard_map/all_to_all | solution.py:395
  122.1 41.0 %attend_backward.1 = bf16[32,144,256]{2,1,0:T(8,128)(2,1)} custom-call(s32[4]{0:T(128)} %slice_reduce_fusion.refs_0_, s32[32]{0:T(128)} %fusion.9.refs_2_.refs_1_, s32[32]{0:T(128)} %xor.16.refs_1_.refs_3_.refs_2_, s32[32]{0:T(128)} %copy-done.14, bf16[4,1168,128]{2,1,0:T(8,128)(2,1)} %copy-done, bf16[256,128]{1,0:T(8,128)(2,1)} %copy-done.4, ...), custom_call_target="tpu_custom_call" | custom-call | flops 34359738368 | bytes 1048576 | tf_op jit(solution)/shard_map/attend_backward/pallas_call | solution.py:263
  163.2 12.3 %all-to-all-done = bf16[32,144,256]{2,1,0:T(8,128)(2,1)S(1)} async-done(((bf16[32,144,256]{2,1,0:T(8,128)(2,1)}), bf16[32,144,256]{2,1,0:T(8,128)(2,1)S(1)}, u32[]{:S(2)}, u32[]{:S(2)}) %all-to-all-start) | async-done | bytes 2359328 | tf_op jit(solution)/shard_map/all_to_all | solution.py:395
  176.9 17.2 %all-to-all-start.1 = ((bf16[32,144,256]{2,1,0:T(8,128)(2,1)}), bf16[32,144,256]{2,1,0:T(8,128)(2,1)}, u32[]{:S(2)}, u32[]{:S(2)}) async-start(bf16[32,144,256]{2,1,0:T(8,128)(2,1)} %attend_backward.1), calls=%async_computation.1 | async-start | bytes 4718592 | tf_op jit(solution)/shard_map/all_to_all | solution.py:396
  194.7 28.5 %all-to-all-done.1 = bf16[32,144,256]{2,1,0:T(8,128)(2,1)} async-done(((bf16[32,144,256]{2,1,0:T(8,128)(2,1)}), bf16[32,144,256]{2,1,0:T(8,128)(2,1)}, u32[]{:S(2)}, u32[]{:S(2)}) %all-to-all-start.1) | async-done | bytes 2359328 | tf_op jit(solution)/shard_map/all_to_all | solution.py:396
  223.2 5.1 %merge.1 = bf16[4,128,256]{2,1,0:T(8,128)(2,1)} custom-call(s32[1]{0:T(128)} %bitcast.1.place, bf16[8,4,144,256]{3,2,1,0:T(8,128)(2,1)} %bitcast.35, bf16[8,4,144,256]{3,2,1,0:T(8,128)(2,1)} %bitcast.13.cols, bf16[4,144,256]{2,1,0:T(8,128)(2,1)} %copy-done.2, f32[1,256]{1,0:T(1,128)} %constant_dynamic-slice_fusion.bias), custom_call_target="tpu_custom_call" | custom-call | tf_op jit(solution)/shard_map/merge/pallas_call | solution.py:293
  228.3 4.3 %all-to-all-start.2 = ((bf16[4,128,256]{2,1,0:T(8,128)(2,1)}), bf16[4,128,256]{2,1,0:T(8,128)(2,1)S(1)}, u32[]{:S(2)}, u32[]{:S(2)}) async-start(bf16[4,128,256]{2,1,0:T(8,128)(2,1)} %merge.1), calls=%async_computation.2 | async-start | bytes 524288 | tf_op jit(solution)/shard_map/all_to_all | solution.py:399
  232.7 7.5 %all-to-all-done.2 = bf16[4,128,256]{2,1,0:T(8,128)(2,1)S(1)} async-done(((bf16[4,128,256]{2,1,0:T(8,128)(2,1)}), bf16[4,128,256]{2,1,0:T(8,128)(2,1)S(1)}, u32[]{:S(2)}, u32[]{:S(2)}) %all-to-all-start.2) | async-done | bytes 262176 | tf_op jit(solution)/shard_map/all_to_all | solution.py:399
  (108 shorter events, 21.0 us)
Async XLA Ops:
  6.5 63.4 %all-gather.3.cloned.1.call-start = ((), (), s32[]{:S(2)}) async-start(), calls=%async_computation.3 | async-start | bytes 2359296 | tf_op jit(solution)/shard_map/all_gather | solution.py:366
  11.4 7.5 %collective-permute-start.3 = (bf16[272,256]{1,0:T(8,128)(2,1)}, bf16[272,256]{1,0:T(8,128)(2,1)S(1)}, u32[]{:S(2)}, u32[]{:S(2)}) collective-permute-start(bf16[272,256]{1,0:T(8,128)(2,1)} %get-tuple-element.39), channel_id=1, source_target_pairs={{0,1},{1,0},{16,17},{17,16},{2,3},{3,2},{18,19},{19,18},{4,5},{5,4... | collective-permute-start | bytes 417800 | tf_op jit(solution)/shard_map/ppermute | solution.py:331
  14.5 4.4 %collective-permute-start.4 = (bf16[272,256]{1,0:T(8,128)(2,1)}, bf16[272,256]{1,0:T(8,128)(2,1)S(1)}, u32[]{:S(2)}, u32[]{:S(2)}) collective-permute-start(bf16[272,256]{1,0:T(8,128)(2,1)} %get-tuple-element.40), channel_id=1, source_target_pairs={{0,16},{1,17},{16,0},{17,1},{2,18},{3,19},{18,2},{19,3},{4,20},{5,... | collective-permute-start | bytes 417800 | tf_op jit(solution)/shard_map/ppermute | solution.py:331
  14.5 7.0 %collective-permute-start.5 = (bf16[272,256]{1,0:T(8,128)(2,1)}, bf16[272,256]{1,0:T(8,128)(2,1)S(1)}, u32[]{:S(2)}, u32[]{:S(2)}) collective-permute-start(bf16[272,256]{1,0:T(8,128)(2,1)} %get-tuple-element.41), channel_id=1, source_target_pairs={{0,17},{1,16},{16,1},{17,0},{2,19},{3,18},{18,3},{19,2},{4,21},{5,... | collective-permute-start | bytes 417800 | tf_op jit(solution)/shard_map/ppermute | solution.py:331
  24.2 98.0 %all-gather.5.cloned.1.call-start = ((), (), s32[]{:S(2)}) async-start(), calls=%async_computation.4 | async-start | bytes 2654208 | tf_op jit(solution)/shard_map/all_gather | solution.py:386
  25.2 10.4 %collective-permute-start.2 = (bf16[1168,128]{1,0:T(8,128)(2,1)S(1)}, bf16[1168,128]{1,0:T(8,128)(2,1)S(1)}, u32[]{:S(2)}, u32[]{:S(2)}) collective-permute-start(bf16[1168,128]{1,0:T(8,128)(2,1)S(1)} %get-tuple-element.64), channel_id=1, source_target_pairs={{0,17},{1,16},{16,1},{17,0},{2,19},{3,18},{18,3},{19,2},{4,21},{5,... | collective-permute-start | bytes 897032 | tf_op jit(solution)/shard_map/ppermute | solution.py:331
  27.8 11.0 %collective-permute-start.1 = (bf16[1168,128]{1,0:T(8,128)(2,1)S(1)}, bf16[1168,128]{1,0:T(8,128)(2,1)S(1)}, u32[]{:S(2)}, u32[]{:S(2)}) collective-permute-start(bf16[1168,128]{1,0:T(8,128)(2,1)S(1)} %get-tuple-element.64), channel_id=1, source_target_pairs={{0,16},{1,17},{16,0},{17,1},{2,18},{3,19},{18,2},{19,3},{4,20},{5,... | collective-permute-start | bytes 897032 | tf_op jit(solution)/shard_map/ppermute | solution.py:331
  27.8 15.4 %collective-permute-start = (bf16[1168,128]{1,0:T(8,128)(2,1)S(1)}, bf16[1168,128]{1,0:T(8,128)(2,1)S(1)}, u32[]{:S(2)}, u32[]{:S(2)}) collective-permute-start(bf16[1168,128]{1,0:T(8,128)(2,1)S(1)} %get-tuple-element.64), channel_id=1, source_target_pairs={{0,1},{1,0},{16,17},{17,16},{2,3},{3,2},{18,19},{19,18},{4,5},{5,4... | collective-permute-start | bytes 897032 | tf_op jit(solution)/shard_map/ppermute | solution.py:331
  30.0 22.7 %collective-permute-start.6 = (bf16[4,144,256]{2,1,0:T(8,128)(2,1)S(1)}, bf16[4,144,256]{2,1,0:T(8,128)(2,1)S(1)}, u32[]{:S(2)}, u32[]{:S(2)}) collective-permute-start(bf16[4,144,256]{2,1,0:T(8,128)(2,1)S(1)} %copy-done.3), channel_id=1, source_target_pairs={{0,32},{32,0},{64,96},{96,64},{128,160},{160,128},{192,224},{224,1... | collective-permute-start | bytes 884744 | tf_op jit(solution)/shard_map/ppermute | solution.py:367
  31.3 25.9 %collective-permute-start.7 = (bf16[4,144,256]{2,1,0:T(8,128)(2,1)S(1)}, bf16[4,144,256]{2,1,0:T(8,128)(2,1)S(1)}, u32[]{:S(2)}, u32[]{:S(2)}) collective-permute-start(bf16[4,144,256]{2,1,0:T(8,128)(2,1)S(1)} %copy-done.3), channel_id=1, source_target_pairs={{0,64},{32,96},{64,128},{96,160},{128,192},{160,224},{192,0},{224,... | collective-permute-start | bytes 884744 | tf_op jit(solution)/shard_map/ppermute | solution.py:371
  35.6 26.0 %collective-permute-start.9 = (bf16[4,144,256]{2,1,0:T(8,128)(2,1)S(1)}, bf16[4,144,256]{2,1,0:T(8,128)(2,1)S(1)}, u32[]{:S(2)}, u32[]{:S(2)}) collective-permute-start(bf16[4,144,256]{2,1,0:T(8,128)(2,1)S(1)} %copy-done.3), channel_id=1, source_target_pairs={{0,128},{32,160},{64,192},{96,224},{128,0},{160,32},{192,64},{224,... | collective-permute-start | bytes 884744 | tf_op jit(solution)/shard_map/ppermute | solution.py:371
  38.8 22.8 %collective-permute-start.11 = (bf16[4,144,256]{2,1,0:T(8,128)(2,1)S(1)}, bf16[4,144,256]{2,1,0:T(8,128)(2,1)S(1)}, u32[]{:S(2)}, u32[]{:S(2)}) collective-permute-start(bf16[4,144,256]{2,1,0:T(8,128)(2,1)S(1)} %copy-done.3), channel_id=1, source_target_pairs={{0,192},{32,224},{64,0},{96,32},{128,64},{160,96},{192,128},{224,1... | collective-permute-start | bytes 884744 | tf_op jit(solution)/shard_map/ppermute | solution.py:371
  43.2 11.0 %collective-permute-start.13 = (bf16[4,128,256]{2,1,0:T(8,128)(2,1)S(1)}, bf16[4,128,256]{2,1,0:T(8,128)(2,1)S(1)}, u32[]{:S(2)}, u32[]{:S(2)}) collective-permute-start(bf16[4,128,256]{2,1,0:T(8,128)(2,1)S(1)} %copy-done.1), channel_id=1, source_target_pairs={{0,32},{32,0},{64,96},{96,64},{128,160},{160,128},{192,224},{224,1... | collective-permute-start | bytes 786440 | tf_op jit(solution)/shard_map/ppermute | solution.py:368
  52.7 62.6 %copy-start.14 = (s32[32]{0:T(128)}, s32[32]{0:T(128)S(1)}, u32[]{:S(2)}) copy-start(s32[32]{0:T(128)S(1)} %xor.18.refs_3_) | copy-start | bytes 388
  52.7 10.0 %collective-permute-start.8 = (bf16[4,144,256]{2,1,0:T(8,128)(2,1)S(1)}, bf16[4,144,256]{2,1,0:T(8,128)(2,1)S(1)}, u32[]{:S(2)}, u32[]{:S(2)}) collective-permute-start(bf16[4,144,256]{2,1,0:T(8,128)(2,1)S(1)} %collective-permute-done.6.refs_9_), channel_id=1, source_target_pairs={{0,64},{32,96},{64,128},{96,160},{128,192},{160,224},{192,0},{224,... | collective-permute-start | bytes 884744 | tf_op jit(solution)/shard_map/ppermute | solution.py:371
  54.2 15.4 %collective-permute-start.10 = (bf16[4,144,256]{2,1,0:T(8,128)(2,1)S(1)}, bf16[4,144,256]{2,1,0:T(8,128)(2,1)S(1)}, u32[]{:S(2)}, u32[]{:S(2)}) collective-permute-start(bf16[4,144,256]{2,1,0:T(8,128)(2,1)S(1)} %collective-permute-done.6.refs_9_), channel_id=1, source_target_pairs={{0,128},{32,160},{64,192},{96,224},{128,0},{160,32},{192,64},{224,... | collective-permute-start | bytes 884744 | tf_op jit(solution)/shard_map/ppermute | solution.py:371
  57.1 12.8 %collective-permute-start.12 = (bf16[4,144,256]{2,1,0:T(8,128)(2,1)S(1)}, bf16[4,144,256]{2,1,0:T(8,128)(2,1)S(1)}, u32[]{:S(2)}, u32[]{:S(2)}) collective-permute-start(bf16[4,144,256]{2,1,0:T(8,128)(2,1)S(1)} %collective-permute-done.6.refs_9_), channel_id=1, source_target_pairs={{0,192},{32,224},{64,0},{96,32},{128,64},{160,96},{192,128},{224,1... | collective-permute-start | bytes 884744 | tf_op jit(solution)/shard_map/ppermute | solution.py:371
  70.0 45.3 %collective-permute-start.14 = (bf16[8,128,256]{2,1,0:T(8,128)(2,1)}, bf16[8,128,256]{2,1,0:T(8,128)(2,1)S(1)}, u32[]{:S(2)}, u32[]{:S(2)}) collective-permute-start(bf16[8,128,256]{2,1,0:T(8,128)(2,1)} %pair.1.refs_7_), channel_id=1, source_target_pairs={{0,64},{32,96},{64,128},{96,160},{128,192},{160,224},{192,0},{224,... | collective-permute-start | bytes 1572872 | tf_op jit(solution)/shard_map/ppermute | solution.py:387
  71.9 43.4 %collective-permute-start.15 = (bf16[8,128,256]{2,1,0:T(8,128)(2,1)}, bf16[8,128,256]{2,1,0:T(8,128)(2,1)S(1)}, u32[]{:S(2)}, u32[]{:S(2)}) collective-permute-start(bf16[8,128,256]{2,1,0:T(8,128)(2,1)} %pair.1.refs_7_), channel_id=1, source_target_pairs={{0,128},{32,160},{64,192},{96,224},{128,0},{160,32},{192,64},{224,... | collective-permute-start | bytes 1572872 | tf_op jit(solution)/shard_map/ppermute | solution.py:387
  74.3 41.0 %collective-permute-start.16 = (bf16[8,128,256]{2,1,0:T(8,128)(2,1)}, bf16[8,128,256]{2,1,0:T(8,128)(2,1)S(1)}, u32[]{:S(2)}, u32[]{:S(2)}) collective-permute-start(bf16[8,128,256]{2,1,0:T(8,128)(2,1)} %pair.1.refs_7_), channel_id=1, source_target_pairs={{0,192},{32,224},{64,0},{96,32},{128,64},{160,96},{192,128},{224,1... | collective-permute-start | bytes 1572872 | tf_op jit(solution)/shard_map/ppermute | solution.py:387
  116.4 59.1 %all-to-all-start = ((bf16[32,144,256]{2,1,0:T(8,128)(2,1)}), bf16[32,144,256]{2,1,0:T(8,128)(2,1)S(1)}, u32[]{:S(2)}, u32[]{:S(2)}) async-start(bf16[32,144,256]{2,1,0:T(8,128)(2,1)} %attend_forward.1), calls=%async_computation | async-start | bytes 4718592 | tf_op jit(solution)/shard_map/all_to_all | solution.py:395
  163.1 31.0 %copy-start.13 = (f32[1024]{0:T(1024)S(1)}, f32[1024]{0:T(1024)}, u32[]{:S(2)}) copy-start(f32[1024]{0:T(1024)} %param.19) | copy-start | bytes 12292
  176.9 46.2 %all-to-all-start.1 = ((bf16[32,144,256]{2,1,0:T(8,128)(2,1)}), bf16[32,144,256]{2,1,0:T(8,128)(2,1)}, u32[]{:S(2)}, u32[]{:S(2)}) async-start(bf16[32,144,256]{2,1,0:T(8,128)(2,1)} %attend_backward.1), calls=%async_computation.1 | async-start | bytes 4718592 | tf_op jit(solution)/shard_map/all_to_all | solution.py:396
  228.3 11.9 %all-to-all-start.2 = ((bf16[4,128,256]{2,1,0:T(8,128)(2,1)}), bf16[4,128,256]{2,1,0:T(8,128)(2,1)S(1)}, u32[]{:S(2)}, u32[]{:S(2)}) async-start(bf16[4,128,256]{2,1,0:T(8,128)(2,1)} %merge.1), calls=%async_computation.2 | async-start | bytes 524288 | tf_op jit(solution)/shard_map/all_to_all | solution.py:399
  (25 other events, 198.0 us)
Sparse Core Ops, SparseCore 0:
  24.3 41.6 all-gather.2
  75.3 41.5 all-gather.4
where the time goes:
time: 248 us
  Pallas kernels  102 us (41%)
  waiting for transfers between devices  69.3 us (28%)
  starting transfers between devices  53.7 us (22%)
  between operations  14.4 us (6%)
  local copies, waits for them, and re-layouts  7.18 us (3%)
    pallas_call x3, Pallas kernels, attend(): pl.pallas_call(functools.partial(attend_kernel, kind, split), out_shape=j...  87.9 us
    all_to_all x1, waiting for transfers between devices, body(): cols = lax.all_to_all(to_cols, 'R', 0, 0, tiled=True).reshape(8, 4, SRC, HS)  28.5 us
    all_to_all x1, starting transfers between devices, body(): cols = lax.all_to_all(to_cols, 'R', 0, 0, tiled=True).reshape(8, 4, SRC, HS)  17.2 us
    ppermute x6, waiting for transfers between devices, swap(): return lax.ppermute(value, group, [(i, i ^ d) for i in range(4)])  12.5 us
    all_to_all x1, waiting for transfers between devices, body(): rows = lax.all_to_all(to_rows, 'C', 0, 0, tiled=True).reshape(8, 4, SRC, HS)  12.3 us
    ppermute x3, waiting for transfers between devices, body(): lax.ppermute(source_beside, 'R', way)  8.28 us
    all_to_all x1, waiting for transfers between devices, body(): merged = lax.all_to_all(merged, group, 0, 0, tiled=True)  7.53 us
    ppermute x6, starting transfers between devices, swap(): return lax.ppermute(value, group, [(i, i ^ d) for i in range(4)])  7.46 us
  transfers between devices with their start and end apart: 22, of which 10 were waited for; matrix products, arithmetic and copies ran while one was open for 2% of the time, Pallas kernels for 36%

commit v1 on v0

--- a/solution.py
+++ b/solution.py
@@ -150,14 +150,17 @@
     return jnp.where(lane % 2 == 1, planes[2], jnp.where(lane < half, low, high))
 
 
-def attend_kernel(kind, split, *refs):
+def attend_kernel(kind, split, picked, shift, *refs):
+    parts = split[2]
     if kind == "self":
-        target_pieces, source_pieces, (masks, halves, scaled, out, acc, peak, den, minus, wide, planes) = refs[:1], refs[1:2], refs[2:]
+        target_pieces, source_pieces, (masks, halves, scaled, *outs) = refs[:1], refs[1:2], refs[2:]
+        outs, (acc, peak, den, minus, wide, planes) = outs[:parts], outs[parts:]
         targets, sources = target_pieces[0], source_pieces[0]
     else:
-        count, target_at, source_at, out_at, masks, halves, scaled = refs[:7]
-        target_pieces, source_pieces = refs[7 : 7 + split[0]], refs[7 + split[0] : 7 + sum(split)]
-        out, acc, peak, den, minus, wide, planes, targets, sources, sems = refs[7 + sum(split) :]
+        count, target_at, source_at, out_at, pick_at, masks, halves, scaled = refs[:8]
+        target_pieces, source_pieces = refs[8 : 8 + split[0]], refs[8 + split[0] : 8 + sum(split[:2])]
+        rest = refs[8 + sum(split[:2]) :]
+        outs, (acc, peak, den, minus, wide, planes, targets, sources, sems) = rest[:parts], rest[parts:]
     blocks = acc.shape[0]
     copies = []
     if kind != "self":
@@ -219,28 +222,36 @@
                 start = jnp.where(past, end, start)
             slot = i - start
             at = cell * 8 + slot
-            one(cell, slot, target_at[at], source_at[at], out_at[at])
+            pick = pick_at[at]
+
+            @pl.when((pick >= picked[0]) & (pick < picked[1]))
+            def _():
+                one(cell, slot, target_at[at] - shift, source_at[at], out_at[at] - shift)
+
             return carry
 
         lax.fori_loop(0, ends[2] + count[3], step, 0)
 
-    def finish(b, carry):
-        total = jnp.maximum(den[b], 1e-30)
-        inverse = 1.0 / total
-        out[b, :BS, :] = (acc[b] * jnp.concatenate([inverse, inverse], axis=1)).astype(BF16)
-        out[b, BS:, :] = pack_rows((peak[b] + jnp.log(total)).T[0:1])
-        return carry
-
-    lax.fori_loop(0, blocks, finish, 0)
-
-
-def attend(kind, lists, masks, attn, targets, sources):
+    each = blocks // parts
+    for part, out in enumerate(outs):
+
+        def finish(at, carry):
+            b = part * each + at
+            total = jnp.maximum(den[b], 1e-30)
+            inverse = 1.0 / total
+            out[at, :BS, :] = (acc[b] * jnp.concatenate([inverse, inverse], axis=1)).astype(BF16)
+            out[at, BS:, :] = pack_rows((peak[b] + jnp.log(total)).T[0:1])
+            return carry
+
+        lax.fori_loop(0, each, finish, 0)
+
+
+def attend(kind, lists, masks, attn, targets, sources, blocks=4, parts=1, picked=None, shift=0):
     smem = pl.BlockSpec(memory_space=pltpu.SMEM)
     vmem = pl.BlockSpec(memory_space=pltpu.VMEM)
     hbm = pl.BlockSpec(memory_space=pltpu.HBM)
-    split = (len(targets), len(sources))
-    blocks = 4 if kind == "self" else 32
-    slots = 4 if kind == "self" else 16
+    split = (len(targets), len(sources), parts)
+    slots = 4 if kind == "self" else 8
     scratch = [
         pltpu.VMEM((blocks, BS, HS), F32),
         pltpu.VMEM((blocks, BS, BS), F32),
@@ -254,19 +265,21 @@
         specs = [vmem] * 5
     else:
         operands = (*lists, masks, *attn, *targets, *sources)
-        specs = [smem] * 4 + [vmem] * 3 + [hbm] * sum(split)
+        specs = [smem] * 5 + [vmem] * 3 + [hbm] * sum(split[:2])
         scratch += [
-            pltpu.VMEM((blocks, BS, HS), BF16),
-            pltpu.VMEM((blocks, SRC, HS), BF16),
-            pltpu.SemaphoreType.DMA((sum(split),)),
+            pltpu.VMEM((sum(t.shape[0] for t in targets), BS, HS), BF16),
+            pltpu.VMEM((sum(t.shape[0] for t in sources), SRC, HS), BF16),
+            pltpu.SemaphoreType.DMA((sum(split[:2]),)),
         ]
     return pl.pallas_call(
-        functools.partial(attend_kernel, kind, split),
-        out_shape=jax.ShapeDtypeStruct((blocks, SRC, HS), BF16),
+        functools.partial(attend_kernel, kind, split, picked, shift),
+        out_shape=[jax.ShapeDtypeStruct((blocks // parts, SRC, HS), BF16)] * parts,
         in_specs=specs,
-        out_specs=vmem,
+        out_specs=[vmem] * parts,
         scratch_shapes=scratch,
-        compiler_params=pltpu.CompilerParams(vmem_limit_bytes=(16 if kind == "self" else 56) << 20),
+        compiler_params=pltpu.CompilerParams(
+            vmem_limit_bytes=(16 if kind == "self" else 56) << 20
+        ),
         cost_estimate=pl.CostEstimate(
             flops=slots * BS * BS * HS * 512, bytes_accessed=1 << 20, transcendentals=0
         ),
@@ -274,13 +287,14 @@
     )(*operands)
 
 
-def merge_kernel(place, rows, cols, own, bias, out):
-    parts = [rows.at[p, 0] for p in range(8)] + [cols.at[p, 0] for p in range(8)] + [own.at[0]]
+def merge_kernel(place, far, *refs):
+    *single, bias, out = refs
+    parts = [far.at[p, 0] for p in range(8)] + [ref.at[0] for ref in single]
     sums = [unpack_rows(part[BS:SRC, :BS]) for part in parts]
     top = functools.reduce(jnp.maximum, sums)
     shares = [jnp.exp(value - top) for value in sums]
     total = functools.reduce(jnp.add, shares)
-    table = jnp.concatenate([share / total for share in shares] + [jnp.zeros((BS - 17, BS), F32)])
+    table = jnp.concatenate([share / total for share in shares] + [jnp.zeros((BS - len(parts), BS), F32)])
     table = table.T
     result = jnp.zeros((BS, HS), F32)
     for p, part in enumerate(parts):
@@ -288,24 +302,21 @@
     out[0] = (result + bias[...]).astype(BF16)
 
 
-def merge(place, rows, cols, own, bias):
-    blocks = own.shape[0]
+def merge(place, far, single, bias):
+    blocks = single[0].shape[0]
     return pl.pallas_call(
         merge_kernel,
         grid_spec=pltpu.PrefetchScalarGridSpec(
             num_scalar_prefetch=1,
             grid=(blocks,),
-            in_specs=[
-                pl.BlockSpec((8, 1, SRC, HS), lambda d, place: (0, d, 0, 0)),
-                pl.BlockSpec((8, 1, SRC, HS), lambda d, place: (0, d, 0, 0)),
-                pl.BlockSpec((1, SRC, HS), lambda d, place: (d, 0, 0)),
-                pl.BlockSpec((1, HS), lambda d, place: (0, 0)),
-            ],
+            in_specs=[pl.BlockSpec((8, 1, SRC, HS), lambda d, place: (0, d, 0, 0))]
+            + [pl.BlockSpec((1, SRC, HS), lambda d, place: (d, 0, 0))] * len(single)
+            + [pl.BlockSpec((1, HS), lambda d, place: (0, 0))],
             out_specs=pl.BlockSpec((1, BS, HS), lambda d, place: (d ^ place[0], 0, 0)),
         ),
         out_shape=jax.ShapeDtypeStruct((blocks, BS, HS), BF16),
         name="merge",
-    )(place, rows, cols, own, bias)
+    )(place, far, *single, bias)
 
 
 def body(
@@ -331,7 +342,6 @@
         return lax.ppermute(value, group, [(i, i ^ d) for i in range(4)])
 
     sent = project(place, features, node_valid, attn, weight_src, weight_tgt)
-    sent, pair_masks = lax.optimization_barrier((sent, pair_masks))
     mine = [sent[0]] + [swap(d, sent[d]) for d in (1, 2, 3)]
 
     identity = jnp.eye(BS, dtype=bool)
@@ -356,19 +366,30 @@
     from_row = second_at // 4
     y_steps = (me // 2 - from_row // 2) % 4
     x_steps = (me + from_row) % 2
-    second_near = (y_steps * 2 + x_steps) * 4 + second_at % 4
+    second_near = ((y_steps + 3) % 4 * 2 + x_steps) * 4 + second_at % 4
+    z_steps = (lax.axis_index("C") - first_at // 4) % 8
+    first_near = (z_steps + 1) % 8 * 4 + first_at % 4
 
     source, target = gather_square(mine)
 
     size = lax.axis_size("R")
     across = [(i, i ^ 1) for i in range(size)]
     around = [[(i, (i + 2 * k) % size) for i in range(size)] for k in (1, 2, 3)]
+
+    def along_z(step, value):
+        return lax.ppermute(value, "C", [(i, (i + step) % 8) for i in range(8)])
+
     row_targets = lax.all_gather(target, "C", axis=0, tiled=True)
     source_beside = lax.ppermute(source, "R", across)
-    target_beside = lax.ppermute(target, "R", across)
-    col_sources = [source, source_beside]
+    col_sources = []
     for way in around:
         col_sources += [lax.ppermute(source, "R", way), lax.ppermute(source_beside, "R", way)]
+    col_sources += [source, source_beside]
+    near_targets = [along_z(7, target), target, along_z(1, target)]
+    col_sources, near_targets, later_target = lax.optimization_barrier(
+        (col_sources, near_targets, target)
+    )
+    target_beside = lax.ppermute(later_target, "R", across)
 
     scaled = 0.8 * lax.dynamic_index_in_dim(attn, head, 0, keepdims=False)
     high = lax.reduce_precision(scaled, 8, 7)
@@ -378,24 +399,57 @@
     ).astype(BF16)
     shared = (halves, scaled[None])
 
-    own = attend("self", (), cells, shared, [target], [source])
-    both = pair(target, target_beside)
-    (row_targets, *col_sources), both, later_source, own = lax.optimization_barrier(
-        ((row_targets, *col_sources), both, source, own)
+    (own,) = attend("self", (), cells, shared, [target], [source])
+    to_near = attend(
+        "forward",
+        (count, first_near, second_near, first_near, first_near),
+        cells,
+        shared,
+        near_targets,
+        col_sources,
+        blocks=12,
+        parts=3,
+        picked=(0, 12),
+    )
+    both = pair(later_target, target_beside)
+    row_targets, both, later_source, own, to_near = lax.optimization_barrier(
+        (row_targets, both, source, own, to_near)
     )
     row_sources = lax.all_gather(later_source, "C", axis=0, tiled=True)
-    col_targets = [both] + [lax.ppermute(both, "R", way) for way in around]
-    to_rows = attend(
-        "forward", (count, first_at, second_near, first_at), cells, shared, [row_targets], col_sources
-    )
-    to_rows, col_targets = lax.optimization_barrier((to_rows, col_targets))
-    to_cols = attend(
-        "backward", (count, second_near, first_at, second_at), cells, shared, col_targets, [row_sources]
-    )
-    rows = lax.all_to_all(to_rows, "C", 0, 0, tiled=True).reshape(8, 4, SRC, HS)
-    cols = lax.all_to_all(to_cols, "R", 0, 0, tiled=True).reshape(8, 4, SRC, HS)
+    around_targets = [lax.ppermute(both, "R", way) for way in around]
+    (to_far,) = attend(
+        "forward",
+        (count, first_at, second_near, first_at, first_near),
+        cells,
+        shared,
+        [row_targets],
+        col_sources,
+        blocks=32,
+        picked=(12, 32),
+    )
+    near = [along_z(1, to_near[0]), to_near[1], along_z(7, to_near[2])]
+    to_far, around_targets = lax.optimization_barrier((to_far, around_targets))
+    far = lax.all_to_all(to_far, "C", 0, 0, tiled=True).reshape(8, 4, SRC, HS)
+    cols = []
+    for half in range(2):
+        to_cols = attend(
+            "backward",
+            (count, second_near, first_at, second_near, second_near),
+            cells,
+            shared,
+            around_targets[:2] if half == 0 else [around_targets[2], both],
+            [row_sources],
+            blocks=16,
+            parts=4,
+            picked=(16 * half, 16 * half + 16),
+            shift=16 * half,
+        )
+        for part, value in enumerate(to_cols):
+            y_step, x_step = (1, 2, 3, 0)[half * 2 + part // 2], part % 2
+            back = [(i, (i // 2 - y_step) % 4 * 2 + (i % 2 ^ x_step)) for i in range(size)]
+            cols.append(value if y_step == x_step == 0 else lax.ppermute(value, "R", back))
     bias_head = lax.dynamic_index_in_dim(bias.reshape(heads, HS), head, 0)
-    merged = merge(place, rows, cols, own, bias_head)
+    merged = merge(place, far, [*near, *cols, own], bias_head)
     merged = lax.all_to_all(merged, group, 0, 0, tiled=True)
     result = merged.transpose(1, 0, 2).reshape(BS, heads * HS)
     return jnp.where(node_valid[0][:, None] > 0, result, bias.astype(BF16)[None, :])

time: 248 us -> 255 us (1.028); the launches traced: 248 us -> 252 us
  starting transfers between devices: 53.7 us -> 102 us
  Pallas kernels: 102 us -> 72 us
  waiting for transfers between devices: 69.3 us -> 53.8 us
    ppermute x4 -> x15, starting transfers between devices: 6.13 us -> 59.3 us  [the longest x7 38.9 us: body(): lax.ppermute(value, 'R', back)]
    all_to_all x2 -> x1, waiting for transfers between devices: 40.8 us -> 0.01 us  [body(): far = lax.all_to_all(to_far, 'C', 0, 0, tiled=True).reshape(8, 4, SRC, HS)]
    pallas_call x3 -> x5, Pallas kernels: 87.9 us -> 57.8 us  [attend(): pl.pallas_call(functools.partial(attend_kernel, kind, split, picked, shif...]
    all_gather x1, waiting for transfers between devices: 0.01 us -> 15.1 us  [body(): row_sources = lax.all_gather(later_source, 'C', axis=0, tiled=True)]
    ppermute x4 -> x15, waiting for transfers between devices: 0.01 us -> 14.4 us  [the longest x7 13 us: body(): lax.ppermute(value, 'R', back)]
    all_to_all x2 -> x1, starting transfers between devices: 22.9 us -> 13.6 us  [body(): far = lax.all_to_all(to_far, 'C', 0, 0, tiled=True).reshape(8, 4, SRC, HS)]
    ppermute x3, waiting for transfers between devices: 0.01 us -> 8.52 us  [body(): lax.ppermute(source, 'R', way)]
    ppermute x6, waiting for transfers between devices: 12.5 us -> 4.41 us  [swap(): return lax.ppermute(value, group, [(i, i ^ d) for i in range(4)])]
  transfers between devices with their start and end apart: 22 -> 32, of which waited for: 10 -> 10; matrix products, arithmetic and copies ran while one was open for 2% -> 1% of each run, Pallas kernels for 36% -> 24%
where the time goes in v1:
time: 255 us; the launch traced here: 252 us
  starting transfers between devices  102 us (40%)
  Pallas kernels  72 us (28%)
  waiting for transfers between devices  53.8 us (21%)
  between operations  14.5 us (6%)
  local copies, waits for them, and re-layouts  7.29 us (3%)
    pallas_call x5, Pallas kernels, attend(): pl.pallas_call(functools.partial(attend_kernel, kind, split, picked, shif...  57.8 us
    ppermute x7, starting transfers between devices, body(): lax.ppermute(value, 'R', back)  38.9 us
    ppermute x3, starting transfers between devices, body(): around_targets = [lax.ppermute(both, 'R', way) for way in around]  15.2 us
    all_gather x1, waiting for transfers between devices, body(): row_sources = lax.all_gather(later_source, 'C', axis=0, tiled=True)  15.1 us
    all_to_all x1, starting transfers between devices, body(): far = lax.all_to_all(to_far, 'C', 0, 0, tiled=True).reshape(8, 4, SRC, HS)  13.6 us
    ppermute x7, waiting for transfers between devices, body(): lax.ppermute(value, 'R', back)  13 us
    ppermute x6, starting transfers between devices, swap(): return lax.ppermute(value, group, [(i, i ^ d) for i in range(4)])  9.62 us
    ppermute x3, waiting for transfers between devices, body(): lax.ppermute(source, 'R', way)  8.52 us
  transfers between devices with their start and end apart: 32, of which 10 were waited for; matrix products, arithmetic and copies ran while one was open for 1% of the time, Pallas kernels for 24%

profile of v1, /device:TPU:64, one launch (start us, length us, event | category | flops | bytes accessed | tf_op | source)
XLA Modules:
  0.0 251.9 jit_solution(6112476678882405176)
XLA Ops:
  6.5 4.9 %project.1 = (bf16[272,256]{1,0:T(8,128)(2,1)}, bf16[272,256]{1,0:T(8,128)(2,1)}, bf16[272,256]{1,0:T(8,128)(2,1)}, bf16[272,256]{1,0:T(8,128)(2,1)}) custom-call(s32[1]{0:T(128)} %bitcast.1.place, bf16[128,1024]{1,0:T(8,128)(2,1)} %features.1, s32[1,128]{1,0:T(1,128)} %valid.1, f32[4,256]{1,0:T(4,128)} %attn.1, bf16[1024,1024]{1,0:T(8,128)(2,1)} %weight_src.1, ...), custom_call_target="tpu_custom_call" | custom-call | tf_op jit(solution)/shard_map/project/pallas_call | solution.py:62
  11.4 3.0 %collective-permute-start.3 = (bf16[272,256]{1,0:T(8,128)(2,1)}, bf16[272,256]{1,0:T(8,128)(2,1)S(1)}, u32[]{:S(2)}, u32[]{:S(2)}) collective-permute-start(bf16[272,256]{1,0:T(8,128)(2,1)} %get-tuple-element.46), channel_id=1, source_target_pairs={{0,1},{1,0},{16,17},{17,16},{2,3},{3,2},{18,19},{19,18},{4,5},{5,4... | collective-permute-start | bytes 417800 | tf_op jit(solution)/shard_map/ppermute | solution.py:342
  28.0 3.1 %collective-permute-start.9 = (bf16[4,144,256]{2,1,0:T(8,128)(2,1)}, bf16[4,144,256]{2,1,0:T(8,128)(2,1)S(1)}, u32[]{:S(2)}, u32[]{:S(2)}) collective-permute-start(bf16[4,144,256]{2,1,0:T(8,128)(2,1)} %get-tuple-element.74.refs_1_.refs_17_.refs_15_), channel_id=1, source_target_pairs={{0,128},{32,160},{64,192},{96,224},{128,0},{160,32},{192,64},{224,... | collective-permute-start | bytes 884744 | tf_op jit(solution)/shard_map/ppermute | solution.py:386
  31.2 4.4 %collective-permute-done = bf16[1168,128]{1,0:T(8,128)(2,1)S(1)} collective-permute-done((bf16[1168,128]{1,0:T(8,128)(2,1)S(1)}, bf16[1168,128]{1,0:T(8,128)(2,1)S(1)}, u32[]{:S(2)}, u32[]{:S(2)}) %collective-permute-start) | collective-permute-done | bytes 299040 | tf_op jit(solution)/shard_map/ppermute | solution.py:342
  38.6 6.8 %attend_self.1.refs_11_ = bf16[4,144,256]{2,1,0:T(8,128)(2,1)S(1)} custom-call(bf16[4,128,256]{2,1,0:T(8,128)(2,1)S(1)} %copy-done.1, bf16[4,144,256]{2,1,0:T(8,128)(2,1)S(1)} %copy-done.2, bf16[4,1168,128]{2,1,0:T(8,128)(2,1)S(1)} %pad_maximum_fusion.refs_2_.refs_5_, bf16[256,128]{1,0:T(8,128)(2,1)S(1)} %pad_maximum_fusion.1.refs_3_.refs_6_, ...), custom_call_target="tpu_custom_call" | custom-call | flops 8589934592 | bytes 1048576 | tf_op jit(solution)/shard_map/attend_self/pallas_call | solution.py:274
  46.4 3.1 %collective-permute-start.11 = (bf16[4,144,256]{2,1,0:T(8,128)(2,1)S(1)}, bf16[4,144,256]{2,1,0:T(8,128)(2,1)S(1)}, u32[]{:S(2)}, u32[]{:S(2)}) collective-permute-start(bf16[4,144,256]{2,1,0:T(8,128)(2,1)S(1)} %copy-done.2), channel_id=1, source_target_pairs={{0,192},{32,224},{64,0},{96,32},{128,64},{160,96},{192,128},{224,1... | collective-permute-start | bytes 884744 | tf_op jit(solution)/shard_map/ppermute | solution.py:386
  54.7 8.5 %collective-permute-done.11.refs_15_.refs_13_ = bf16[4,144,256]{2,1,0:T(8,128)(2,1)S(1)} collective-permute-done((bf16[4,144,256]{2,1,0:T(8,128)(2,1)S(1)}, bf16[4,144,256]{2,1,0:T(8,128)(2,1)S(1)}, u32[]{:S(2)}, u32[]{:S(2)}) %collective-permute-start.11) | collective-permute-done | bytes 294944 | tf_op jit(solution)/shard_map/ppermute | solution.py:386
  64.1 2.9 %collective-permute-done.12.refs_16_.refs_14_ = bf16[4,144,256]{2,1,0:T(8,128)(2,1)S(1)} collective-permute-done((bf16[4,144,256]{2,1,0:T(8,128)(2,1)S(1)}, bf16[4,144,256]{2,1,0:T(8,128)(2,1)S(1)}, u32[]{:S(2)}, u32[]{:S(2)}) %collective-permute-start.12) | collective-permute-done | bytes 294944 | tf_op jit(solution)/shard_map/ppermute | solution.py:386
  68.3 8.5 %attend_forward.2 = (bf16[4,144,256]{2,1,0:T(8,128)(2,1)}, bf16[4,144,256]{2,1,0:T(8,128)(2,1)}, bf16[4,144,256]{2,1,0:T(8,128)(2,1)}) custom-call(s32[4]{0:T(128)} %slice_reduce_fusion.refs_0_, s32[32]{0:T(128)} %get-tuple-element.94.refs_1_.refs_3_.refs_4_, s32[32]{0:T(128)} %get-tuple-element.93.refs_2_.refs_1_.refs_3_.refs_4_, ...), custom_call_target="tpu_custom_call" | custom-call | flops 17179869184 | bytes 1048576 | tf_op jit(solution)/shard_map/attend_forward/pallas_call | solution.py:274
  79.5 9.2 %collective-permute-start.16 = (bf16[8,128,256]{2,1,0:T(8,128)(2,1)}, bf16[8,128,256]{2,1,0:T(8,128)(2,1)S(1)}, u32[]{:S(2)}, u32[]{:S(2)}) collective-permute-start(bf16[8,128,256]{2,1,0:T(8,128)(2,1)} %pair.1.refs_9_), channel_id=1, source_target_pairs={{0,64},{32,96},{64,128},{96,160},{128,192},{160,224},{192,0},{224,... | collective-permute-start | bytes 1572872 | tf_op jit(solution)/shard_map/ppermute | solution.py:419
  88.7 3.4 %collective-permute-start.17 = (bf16[8,128,256]{2,1,0:T(8,128)(2,1)}, bf16[8,128,256]{2,1,0:T(8,128)(2,1)}, u32[]{:S(2)}, u32[]{:S(2)}) collective-permute-start(bf16[8,128,256]{2,1,0:T(8,128)(2,1)} %pair.1.refs_9_), channel_id=1, source_target_pairs={{0,128},{32,160},{64,192},{96,224},{128,0},{160,32},{192,64},{224,... | collective-permute-start | bytes 1572872 | tf_op jit(solution)/shard_map/ppermute | solution.py:419
  94.6 17.6 %attend_forward.3 = bf16[32,144,256]{2,1,0:T(8,128)(2,1)} custom-call(s32[4]{0:T(128)} %slice_reduce_fusion.refs_0_, s32[32]{0:T(128)} %copy-done.18, s32[32]{0:T(128)} %get-tuple-element.93.refs_2_.refs_1_.refs_3_.refs_4_, s32[32]{0:T(128)} %copy-done.18, s32[32]{0:T(128)} %get-tuple-element.94.refs_1_.refs_3_.refs_4_, bf16[4,1168,128]{2,1,0:T(8,128)(2,1)} %copy-done, ...), custom_call_target="tpu_custom_call" | custom-call | flops 17179869184 | bytes 1048576 | tf_op jit(solution)/shard_map/attend_forward/pallas_call | solution.py:274
  113.7 13.6 %all-to-all-start = ((bf16[32,144,256]{2,1,0:T(8,128)(2,1)}), bf16[32,144,256]{2,1,0:T(8,128)(2,1)S(1)}, u32[]{:S(2)}, u32[]{:S(2)}) async-start(bf16[32,144,256]{2,1,0:T(8,128)(2,1)} %attend_forward.3), calls=%async_computation | async-start | bytes 4718592 | tf_op jit(solution)/shard_map/all_to_all | solution.py:432
  129.3 15.1 %all-gather.5.cloned.1.call-done.refs_10_ = bf16[32,144,256]{2,1,0:T(8,128)(2,1)} async-done(((bf16[4,144,256]{2,1,0:T(8,128)(2,1)}), bf16[32,144,256]{2,1,0:T(8,128)(2,1)}) %all-gather.5.cloned.1.call-update) | async-done | bytes 2359312 | tf_op jit(solution)/shard_map/all_gather | solution.py:418
  144.4 12.4 %attend_backward.2 = (bf16[4,144,256]{2,1,0:T(8,128)(2,1)}, bf16[4,144,256]{2,1,0:T(8,128)(2,1)}, bf16[4,144,256]{2,1,0:T(8,128)(2,1)}, bf16[4,144,256]{2,1,0:T(8,128)(2,1)}) custom-call(s32[4]{0:T(128)} %slice_reduce_fusion.refs_0_, s32[32]{0:T(128)} %get-tuple-element.93.refs_2_.refs_1_.refs_3_.refs_4_, s32[32]{0:T(128)} %copy-done.18, ...), custom_call_target="tpu_custom_call" | custom-call | flops 17179869184 | bytes 1048576 | tf_op jit(solution)/shard_map/attend_backward/pallas_call | solution.py:274
  157.2 12.1 %collective-permute-start.22 = (bf16[4,144,256]{2,1,0:T(8,128)(2,1)}, bf16[4,144,256]{2,1,0:T(8,128)(2,1)S(1)}, u32[]{:S(2)}, u32[]{:S(2)}) collective-permute-start(bf16[4,144,256]{2,1,0:T(8,128)(2,1)} %get-tuple-element.76), channel_id=1, source_target_pairs={{0,224},{32,192},{64,32},{96,0},{128,96},{160,64},{192,160},{224,1... | collective-permute-start | bytes 884744 | tf_op jit(solution)/shard_map/ppermute | solution.py:450
  169.3 13.0 %collective-permute-start.23 = (bf16[4,144,256]{2,1,0:T(8,128)(2,1)}, bf16[4,144,256]{2,1,0:T(8,128)(2,1)}, u32[]{:S(2)}, u32[]{:S(2)}) collective-permute-start(bf16[4,144,256]{2,1,0:T(8,128)(2,1)} %get-tuple-element.77), channel_id=1, source_target_pairs={{0,128},{32,160},{64,192},{96,224},{128,0},{160,32},{192,64},{224,... | collective-permute-start | bytes 884744 | tf_op jit(solution)/shard_map/ppermute | solution.py:450
  182.3 12.4 %attend_backward.3 = (bf16[4,144,256]{2,1,0:T(8,128)(2,1)}, bf16[4,144,256]{2,1,0:T(8,128)(2,1)}, bf16[4,144,256]{2,1,0:T(8,128)(2,1)}, bf16[4,144,256]{2,1,0:T(8,128)(2,1)}) custom-call(s32[4]{0:T(128)} %slice_reduce_fusion.refs_0_, s32[32]{0:T(128)} %get-tuple-element.93.refs_2_.refs_1_.refs_3_.refs_4_, s32[32]{0:T(128)} %copy-done.18, ...), custom_call_target="tpu_custom_call" | custom-call | flops 17179869184 | bytes 1048576 | tf_op jit(solution)/shard_map/attend_backward/pallas_call | solution.py:274
  194.8 13.2 %collective-permute-start.24 = (bf16[4,144,256]{2,1,0:T(8,128)(2,1)}, bf16[4,144,256]{2,1,0:T(8,128)(2,1)}, u32[]{:S(2)}, u32[]{:S(2)}) collective-permute-start(bf16[4,144,256]{2,1,0:T(8,128)(2,1)} %get-tuple-element.78), channel_id=1, source_target_pairs={{0,160},{32,128},{64,224},{96,192},{128,32},{160,0},{192,96},{224,... | collective-permute-start | bytes 884744 | tf_op jit(solution)/shard_map/ppermute | solution.py:450
  208.9 7.4 %collective-permute-done.24.refs_6_ = bf16[4,144,256]{2,1,0:T(8,128)(2,1)} collective-permute-done((bf16[4,144,256]{2,1,0:T(8,128)(2,1)}, bf16[4,144,256]{2,1,0:T(8,128)(2,1)}, u32[]{:S(2)}, u32[]{:S(2)}) %collective-permute-start.24) | collective-permute-done | bytes 294944 | tf_op jit(solution)/shard_map/ppermute | solution.py:450
  216.3 4.6 %collective-permute-done.25.refs_7_ = bf16[4,144,256]{2,1,0:T(8,128)(2,1)} collective-permute-done((bf16[4,144,256]{2,1,0:T(8,128)(2,1)}, bf16[4,144,256]{2,1,0:T(8,128)(2,1)}, u32[]{:S(2)}, u32[]{:S(2)}) %collective-permute-start.25) | collective-permute-done | bytes 294944 | tf_op jit(solution)/shard_map/ppermute | solution.py:450
  223.3 5.6 %merge.1 = bf16[4,128,256]{2,1,0:T(8,128)(2,1)} custom-call(s32[1]{0:T(128)} %bitcast.1.place, bf16[8,4,144,256]{3,2,1,0:T(8,128)(2,1)} %bitcast.34, bf16[4,144,256]{2,1,0:T(8,128)(2,1)} %copy-done.8, bf16[4,144,256]{2,1,0:T(8,128)(2,1)} %get-tuple-element.70.refs_1_, bf16[4,144,256]{2,1,0:T(8,128)(2,1)} %copy-done.9, bf16[4,144,256]{2,1,0:T(8,128)(2,1)} %copy-done.10, ...), custom_call_target="tpu_custom_call" | custom-call | tf_op jit(solution)/shard_map/merge/pallas_call | solution.py:307
  228.9 7.4 %all-to-all-start.1 = ((bf16[4,128,256]{2,1,0:T(8,128)(2,1)}), bf16[4,128,256]{2,1,0:T(8,128)(2,1)S(1)}, u32[]{:S(2)}, u32[]{:S(2)}) async-start(bf16[4,128,256]{2,1,0:T(8,128)(2,1)} %merge.1), calls=%async_computation.1 | async-start | bytes 524288 | tf_op jit(solution)/shard_map/all_to_all | solution.py:453
  236.3 7.5 %all-to-all-done.1 = bf16[4,128,256]{2,1,0:T(8,128)(2,1)S(1)} async-done(((bf16[4,128,256]{2,1,0:T(8,128)(2,1)}), bf16[4,128,256]{2,1,0:T(8,128)(2,1)S(1)}, u32[]{:S(2)}, u32[]{:S(2)}) %all-to-all-start.1) | async-done | bytes 262176 | tf_op jit(solution)/shard_map/all_to_all | solution.py:453
  (138 shorter events, 37.5 us)
Async XLA Ops:
  6.5 72.9 %all-gather.3.cloned.1.call-start = ((), (), s32[]{:S(2)}) async-start(), calls=%async_computation.2 | async-start | bytes 2359296 | tf_op jit(solution)/shard_map/all_gather | solution.py:382
  20.0 15.6 %collective-permute-start = (bf16[1168,128]{1,0:T(8,128)(2,1)S(1)}, bf16[1168,128]{1,0:T(8,128)(2,1)S(1)}, u32[]{:S(2)}, u32[]{:S(2)}) collective-permute-start(bf16[1168,128]{1,0:T(8,128)(2,1)S(1)} %get-tuple-element.88), channel_id=1, source_target_pairs={{0,1},{1,0},{16,17},{17,16},{2,3},{3,2},{18,19},{19,18},{4,5},{5,4... | collective-permute-start | bytes 897032 | tf_op jit(solution)/shard_map/ppermute | solution.py:342
  25.4 119.0 %all-gather.5.cloned.1.call-start = ((), (), s32[]{:S(2)}) async-start(), calls=%async_computation.3 | async-start | bytes 2654208 | tf_op jit(solution)/shard_map/all_gather | solution.py:418
  25.8 25.9 %collective-permute-start.6 = (bf16[4,144,256]{2,1,0:T(8,128)(2,1)}, bf16[4,144,256]{2,1,0:T(8,128)(2,1)S(1)}, u32[]{:S(2)}, u32[]{:S(2)}) collective-permute-start(bf16[4,144,256]{2,1,0:T(8,128)(2,1)} %get-tuple-element.74.refs_1_.refs_17_.refs_15_), channel_id=1, source_target_pairs={{0,64},{32,96},{64,128},{96,160},{128,192},{160,224},{192,0},{224,... | collective-permute-start | bytes 884744 | tf_op jit(solution)/shard_map/ppermute | solution.py:386
  27.5 22.0 %collective-permute-start.7 = (bf16[4,144,256]{2,1,0:T(8,128)(2,1)}, bf16[4,144,256]{2,1,0:T(8,128)(2,1)S(1)}, u32[]{:S(2)}, u32[]{:S(2)}) collective-permute-start(bf16[4,144,256]{2,1,0:T(8,128)(2,1)} %get-tuple-element.74.refs_1_.refs_17_.refs_15_), channel_id=1, source_target_pairs={{0,32},{32,0},{64,96},{96,64},{128,160},{160,128},{192,224},{224,1... | collective-permute-start | bytes 884744 | tf_op jit(solution)/shard_map/ppermute | solution.py:383
  28.0 26.8 %collective-permute-start.9 = (bf16[4,144,256]{2,1,0:T(8,128)(2,1)}, bf16[4,144,256]{2,1,0:T(8,128)(2,1)S(1)}, u32[]{:S(2)}, u32[]{:S(2)}) collective-permute-start(bf16[4,144,256]{2,1,0:T(8,128)(2,1)} %get-tuple-element.74.refs_1_.refs_17_.refs_15_), channel_id=1, source_target_pairs={{0,128},{32,160},{64,192},{96,224},{128,0},{160,32},{192,64},{224,... | collective-permute-start | bytes 884744 | tf_op jit(solution)/shard_map/ppermute | solution.py:386
  31.1 15.3 %collective-permute-start.13 = (bf16[4,128,256]{2,1,0:T(8,128)(2,1)}, bf16[4,128,256]{2,1,0:T(8,128)(2,1)S(1)}, u32[]{:S(2)}, u32[]{:S(2)}) collective-permute-start(bf16[4,128,256]{2,1,0:T(8,128)(2,1)} %get-tuple-element.53.first.refs_0_.refs_9_), channel_id=1, source_target_pairs={{0,14},{2,0},{4,2},{6,4},{8,6},{10,8},{12,10},{14,12},{1,15},{3,1}... | collective-permute-start | bytes 786440 | tf_op jit(solution)/shard_map/ppermute | solution.py:380
  35.6 13.9 %collective-permute-start.14 = (bf16[4,128,256]{2,1,0:T(8,128)(2,1)}, bf16[4,128,256]{2,1,0:T(8,128)(2,1)S(1)}, u32[]{:S(2)}, u32[]{:S(2)}) collective-permute-start(bf16[4,128,256]{2,1,0:T(8,128)(2,1)} %get-tuple-element.53.first.refs_0_.refs_9_), channel_id=1, source_target_pairs={{0,2},{2,4},{4,6},{6,8},{8,10},{10,12},{12,14},{14,0},{1,3},{3,5},... | collective-permute-start | bytes 786440 | tf_op jit(solution)/shard_map/ppermute | solution.py:380
  46.4 16.9 %collective-permute-start.11 = (bf16[4,144,256]{2,1,0:T(8,128)(2,1)S(1)}, bf16[4,144,256]{2,1,0:T(8,128)(2,1)S(1)}, u32[]{:S(2)}, u32[]{:S(2)}) collective-permute-start(bf16[4,144,256]{2,1,0:T(8,128)(2,1)S(1)} %copy-done.2), channel_id=1, source_target_pairs={{0,192},{32,224},{64,0},{96,32},{128,64},{160,96},{192,128},{224,1... | collective-permute-start | bytes 884744 | tf_op jit(solution)/shard_map/ppermute | solution.py:386
  49.5 14.7 %collective-permute-start.8 = (bf16[4,144,256]{2,1,0:T(8,128)(2,1)S(1)}, bf16[4,144,256]{2,1,0:T(8,128)(2,1)S(1)}, u32[]{:S(2)}, u32[]{:S(2)}) collective-permute-start(bf16[4,144,256]{2,1,0:T(8,128)(2,1)S(1)} %collective-permute-done.7.refs_18_.refs_16_), channel_id=1, source_target_pairs={{0,64},{32,96},{64,128},{96,160},{128,192},{160,224},{192,0},{224,... | collective-permute-start | bytes 884744 | tf_op jit(solution)/shard_map/ppermute | solution.py:386
  49.5 14.6 %collective-permute-start.10 = (bf16[4,144,256]{2,1,0:T(8,128)(2,1)S(1)}, bf16[4,144,256]{2,1,0:T(8,128)(2,1)S(1)}, u32[]{:S(2)}, u32[]{:S(2)}) collective-permute-start(bf16[4,144,256]{2,1,0:T(8,128)(2,1)S(1)} %collective-permute-done.7.refs_18_.refs_16_), channel_id=1, source_target_pairs={{0,128},{32,160},{64,192},{96,224},{128,0},{160,32},{192,64},{224,... | collective-permute-start | bytes 884744 | tf_op jit(solution)/shard_map/ppermute | solution.py:386
  51.7 15.3 %collective-permute-start.12 = (bf16[4,144,256]{2,1,0:T(8,128)(2,1)S(1)}, bf16[4,144,256]{2,1,0:T(8,128)(2,1)S(1)}, u32[]{:S(2)}, u32[]{:S(2)}) collective-permute-start(bf16[4,144,256]{2,1,0:T(8,128)(2,1)S(1)} %collective-permute-done.7.refs_18_.refs_16_), channel_id=1, source_target_pairs={{0,192},{32,224},{64,0},{96,32},{128,64},{160,96},{192,128},{224,1... | collective-permute-start | bytes 884744 | tf_op jit(solution)/shard_map/ppermute | solution.py:386
  79.5 32.8 %collective-permute-start.16 = (bf16[8,128,256]{2,1,0:T(8,128)(2,1)}, bf16[8,128,256]{2,1,0:T(8,128)(2,1)S(1)}, u32[]{:S(2)}, u32[]{:S(2)}) collective-permute-start(bf16[8,128,256]{2,1,0:T(8,128)(2,1)} %pair.1.refs_9_), channel_id=1, source_target_pairs={{0,64},{32,96},{64,128},{96,160},{128,192},{160,224},{192,0},{224,... | collective-permute-start | bytes 1572872 | tf_op jit(solution)/shard_map/ppermute | solution.py:419
  88.7 25.0 %collective-permute-start.17 = (bf16[8,128,256]{2,1,0:T(8,128)(2,1)}, bf16[8,128,256]{2,1,0:T(8,128)(2,1)}, u32[]{:S(2)}, u32[]{:S(2)}) collective-permute-start(bf16[8,128,256]{2,1,0:T(8,128)(2,1)} %pair.1.refs_9_), channel_id=1, source_target_pairs={{0,128},{32,160},{64,192},{96,224},{128,0},{160,32},{192,64},{224,... | collective-permute-start | bytes 1572872 | tf_op jit(solution)/shard_map/ppermute | solution.py:419
  92.1 21.6 %collective-permute-start.18 = (bf16[8,128,256]{2,1,0:T(8,128)(2,1)}, bf16[8,128,256]{2,1,0:T(8,128)(2,1)}, u32[]{:S(2)}, u32[]{:S(2)}) collective-permute-start(bf16[8,128,256]{2,1,0:T(8,128)(2,1)} %pair.1.refs_9_), channel_id=1, source_target_pairs={{0,192},{32,224},{64,0},{96,32},{128,64},{160,96},{192,128},{224,1... | collective-permute-start | bytes 1572872 | tf_op jit(solution)/shard_map/ppermute | solution.py:419
  113.7 108.2 %all-to-all-start = ((bf16[32,144,256]{2,1,0:T(8,128)(2,1)}), bf16[32,144,256]{2,1,0:T(8,128)(2,1)S(1)}, u32[]{:S(2)}, u32[]{:S(2)}) async-start(bf16[32,144,256]{2,1,0:T(8,128)(2,1)} %attend_forward.3), calls=%async_computation | async-start | bytes 4718592 | tf_op jit(solution)/shard_map/all_to_all | solution.py:432
  127.3 67.5 %collective-permute-start.19 = (bf16[4,144,256]{2,1,0:T(8,128)(2,1)}, bf16[4,144,256]{2,1,0:T(8,128)(2,1)S(1)}, u32[]{:S(2)}, u32[]{:S(2)}) collective-permute-start(bf16[4,144,256]{2,1,0:T(8,128)(2,1)} %get-tuple-element.69), channel_id=1, source_target_pairs={{0,2},{2,4},{4,6},{6,8},{8,10},{10,12},{12,14},{14,0},{1,3},{3,5},... | collective-permute-start | bytes 884744 | tf_op jit(solution)/shard_map/ppermute | solution.py:380
  128.8 79.2 %collective-permute-start.20 = (bf16[4,144,256]{2,1,0:T(8,128)(2,1)}, bf16[4,144,256]{2,1,0:T(8,128)(2,1)S(1)}, u32[]{:S(2)}, u32[]{:S(2)}) collective-permute-start(bf16[4,144,256]{2,1,0:T(8,128)(2,1)} %get-tuple-element.71), channel_id=1, source_target_pairs={{0,14},{2,0},{4,2},{6,4},{8,6},{10,8},{12,10},{14,12},{1,15},{3,1}... | collective-permute-start | bytes 884744 | tf_op jit(solution)/shard_map/ppermute | solution.py:380
  156.8 51.2 %collective-permute-start.21 = (bf16[4,144,256]{2,1,0:T(8,128)(2,1)}, bf16[4,144,256]{2,1,0:T(8,128)(2,1)S(1)}, u32[]{:S(2)}, u32[]{:S(2)}) collective-permute-start(bf16[4,144,256]{2,1,0:T(8,128)(2,1)} %get-tuple-element.75), channel_id=1, source_target_pairs={{0,192},{32,224},{64,0},{96,32},{128,64},{160,96},{192,128},{224,1... | collective-permute-start | bytes 884744 | tf_op jit(solution)/shard_map/ppermute | solution.py:450
  157.2 50.9 %collective-permute-start.22 = (bf16[4,144,256]{2,1,0:T(8,128)(2,1)}, bf16[4,144,256]{2,1,0:T(8,128)(2,1)S(1)}, u32[]{:S(2)}, u32[]{:S(2)}) collective-permute-start(bf16[4,144,256]{2,1,0:T(8,128)(2,1)} %get-tuple-element.76), channel_id=1, source_target_pairs={{0,224},{32,192},{64,32},{96,0},{128,96},{160,64},{192,160},{224,1... | collective-permute-start | bytes 884744 | tf_op jit(solution)/shard_map/ppermute | solution.py:450
  169.3 39.6 %collective-permute-start.23 = (bf16[4,144,256]{2,1,0:T(8,128)(2,1)}, bf16[4,144,256]{2,1,0:T(8,128)(2,1)}, u32[]{:S(2)}, u32[]{:S(2)}) collective-permute-start(bf16[4,144,256]{2,1,0:T(8,128)(2,1)} %get-tuple-element.77), channel_id=1, source_target_pairs={{0,128},{32,160},{64,192},{96,224},{128,0},{160,32},{192,64},{224,... | collective-permute-start | bytes 884744 | tf_op jit(solution)/shard_map/ppermute | solution.py:450
  194.8 21.6 %collective-permute-start.24 = (bf16[4,144,256]{2,1,0:T(8,128)(2,1)}, bf16[4,144,256]{2,1,0:T(8,128)(2,1)}, u32[]{:S(2)}, u32[]{:S(2)}) collective-permute-start(bf16[4,144,256]{2,1,0:T(8,128)(2,1)} %get-tuple-element.78), channel_id=1, source_target_pairs={{0,160},{32,128},{64,224},{96,192},{128,32},{160,0},{192,96},{224,... | collective-permute-start | bytes 884744 | tf_op jit(solution)/shard_map/ppermute | solution.py:450
  208.1 13.8 %collective-permute-start.27 = (bf16[4,144,256]{2,1,0:T(8,128)(2,1)}, bf16[4,144,256]{2,1,0:T(8,128)(2,1)}, u32[]{:S(2)}, u32[]{:S(2)}) collective-permute-start(bf16[4,144,256]{2,1,0:T(8,128)(2,1)} %get-tuple-element.83), channel_id=1, source_target_pairs={{0,32},{32,0},{64,96},{96,64},{128,160},{160,128},{192,224},{224,1... | collective-permute-start | bytes 884744 | tf_op jit(solution)/shard_map/ppermute | solution.py:450
  228.9 14.9 %all-to-all-start.1 = ((bf16[4,128,256]{2,1,0:T(8,128)(2,1)}), bf16[4,128,256]{2,1,0:T(8,128)(2,1)S(1)}, u32[]{:S(2)}, u32[]{:S(2)}) async-start(bf16[4,128,256]{2,1,0:T(8,128)(2,1)} %merge.1), calls=%async_computation.1 | async-start | bytes 524288 | tf_op jit(solution)/shard_map/all_to_all | solution.py:453
  (39 other events, 397.6 us)
Sparse Core Ops, SparseCore 0:
  25.5 45.1 all-gather.2
  79.6 64.7 all-gather.4

commit v2 on v1

--- a/solution.py
+++ b/solution.py
@@ -181,7 +181,7 @@
         den[b] = jnp.zeros((BS, BS), F32)
         return carry
 
-    lax.fori_loop(0, blocks, clear, 0)
+    lax.fori_loop(0, blocks, clear, 0, unroll=4)
     for copy in copies:
         copy.wait()
 
@@ -243,7 +243,7 @@
             out[at, BS:, :] = pack_rows((peak[b] + jnp.log(total)).T[0:1])
             return carry
 
-        lax.fori_loop(0, each, finish, 0)
+        lax.fori_loop(0, each, finish, 0, unroll=4)
 
 
 def attend(kind, lists, masks, attn, targets, sources, blocks=4, parts=1, picked=None, shift=0):
@@ -399,7 +399,6 @@
     ).astype(BF16)
     shared = (halves, scaled[None])
 
-    (own,) = attend("self", (), cells, shared, [target], [source])
     to_near = attend(
         "forward",
         (count, first_near, second_near, first_near, first_near),
@@ -412,8 +411,8 @@
         picked=(0, 12),
     )
     both = pair(later_target, target_beside)
-    row_targets, both, later_source, own, to_near = lax.optimization_barrier(
-        (row_targets, both, source, own, to_near)
+    row_targets, both, later_source, to_near = lax.optimization_barrier(
+        (row_targets, both, source, to_near)
     )
     row_sources = lax.all_gather(later_source, "C", axis=0, tiled=True)
     around_targets = [lax.ppermute(both, "R", way) for way in around]
@@ -430,24 +429,29 @@
     near = [along_z(1, to_near[0]), to_near[1], along_z(7, to_near[2])]
     to_far, around_targets = lax.optimization_barrier((to_far, around_targets))
     far = lax.all_to_all(to_far, "C", 0, 0, tiled=True).reshape(8, 4, SRC, HS)
-    cols = []
+    cols, column_targets = [], [around_targets[:2], [around_targets[2], both]]
     for half in range(2):
         to_cols = attend(
             "backward",
             (count, second_near, first_at, second_near, second_near),
             cells,
             shared,
-            around_targets[:2] if half == 0 else [around_targets[2], both],
+            column_targets[half],
             [row_sources],
             blocks=16,
             parts=4,
             picked=(16 * half, 16 * half + 16),
             shift=16 * half,
         )
+        to_cols, near, cols, column_targets[1] = lax.optimization_barrier(
+            (to_cols, near, cols, column_targets[1])
+        )
         for part, value in enumerate(to_cols):
             y_step, x_step = (1, 2, 3, 0)[half * 2 + part // 2], part % 2
             back = [(i, (i // 2 - y_step) % 4 * 2 + (i % 2 ^ x_step)) for i in range(size)]
             cols.append(value if y_step == x_step == 0 else lax.ppermute(value, "R", back))
+    target, to_cols = lax.optimization_barrier((target, to_cols))
+    (own,) = attend("self", (), cells, shared, [target], [source])
     bias_head = lax.dynamic_index_in_dim(bias.reshape(heads, HS), head, 0)
     merged = merge(place, far, [*near, *cols, own], bias_head)
     merged = lax.all_to_all(merged, group, 0, 0, tiled=True)

time: 255 us -> 275 us (1.078)
  waiting for transfers between devices: 53.8 us -> 113 us
  starting transfers between devices: 102 us -> 74.6 us
  Pallas kernels: 72 us -> 60.4 us
    ppermute x4, waiting for transfers between devices: 0.01 us -> 33.9 us  [along_z(): return lax.ppermute(value, 'C', [(i, (i + step) % 8) for i in range(8)])]
    ppermute x7, starting transfers between devices: 38.9 us -> 15.4 us  [body(): lax.ppermute(value, 'R', back)]
    pallas_call x5, Pallas kernels: 57.8 us -> 46.1 us  [attend(): pl.pallas_call(functools.partial(attend_kernel, kind, split, picked, shif...]
    all_gather x1, waiting for transfers between devices: 15.1 us -> 24.6 us  [body(): row_sources = lax.all_gather(later_source, 'C', axis=0, tiled=True)]
    ppermute x6, waiting for transfers between devices: 4.41 us -> 12.1 us  [swap(): return lax.ppermute(value, group, [(i, i ^ d) for i in range(4)])]
    all_to_all x1, starting transfers between devices: 13.6 us -> 20.8 us  [body(): far = lax.all_to_all(to_far, 'C', 0, 0, tiled=True).reshape(8, 4, SRC, HS)]
    ppermute x3, waiting for transfers between devices: 1.44 us -> 8.41 us  [body(): around_targets = [lax.ppermute(both, 'R', way) for way in around]]
    ppermute x3, starting transfers between devices: 15.2 us -> 9.2 us  [body(): around_targets = [lax.ppermute(both, 'R', way) for way in around]]
  transfers between devices with their start and end apart: 32 -> 32, of which waited for: 10 -> 19; matrix products, arithmetic and copies ran while one was open for 1% -> 2% of each run, Pallas kernels for 24% -> 18%
where the time goes in v2:
time: 275 us; the launch traced here: 271 us
  waiting for transfers between devices  113 us (41%)
  starting transfers between devices  74.6 us (27%)
  Pallas kernels  60.4 us (22%)
  between operations  14.5 us (5%)
  local copies, waits for them, and re-layouts  5.7 us (2%)
    pallas_call x5, Pallas kernels, attend(): pl.pallas_call(functools.partial(attend_kernel, kind, split, picked, shif...  46.1 us
    ppermute x4, waiting for transfers between devices, along_z(): return lax.ppermute(value, 'C', [(i, (i + step) % 8) for i in range(8)])  33.9 us
    all_gather x1, waiting for transfers between devices, body(): row_sources = lax.all_gather(later_source, 'C', axis=0, tiled=True)  24.6 us
    all_to_all x1, starting transfers between devices, body(): far = lax.all_to_all(to_far, 'C', 0, 0, tiled=True).reshape(8, 4, SRC, HS)  20.8 us
    ppermute x7, starting transfers between devices, body(): lax.ppermute(value, 'R', back)  15.4 us
    ppermute x7, waiting for transfers between devices, body(): lax.ppermute(value, 'R', back)  14 us
    ppermute x6, waiting for transfers between devices, swap(): return lax.ppermute(value, group, [(i, i ^ d) for i in range(4)])  12.1 us
    ppermute x3, starting transfers between devices, body(): around_targets = [lax.ppermute(both, 'R', way) for way in around]  9.2 us
  transfers between devices with their start and end apart: 32, of which 19 were waited for; matrix products, arithmetic and copies ran while one was open for 2% of the time, Pallas kernels for 18%

profile of v2, /device:TPU:64, one launch (start us, length us, event | category | flops | bytes accessed | tf_op | source)
XLA Modules:
  0.0 270.8 jit_solution(14056050892020245558)
XLA Ops:
  6.5 4.9 %project.1 = (bf16[272,256]{1,0:T(8,128)(2,1)}, bf16[272,256]{1,0:T(8,128)(2,1)}, bf16[272,256]{1,0:T(8,128)(2,1)}, bf16[272,256]{1,0:T(8,128)(2,1)}) custom-call(s32[1]{0:T(128)} %bitcast.1.place, bf16[128,1024]{1,0:T(8,128)(2,1)} %features.1, s32[1,128]{1,0:T(1,128)} %valid.1, f32[4,256]{1,0:T(4,128)} %attn.1, bf16[1024,1024]{1,0:T(8,128)(2,1)} %weight_src.1, ...), custom_call_target="tpu_custom_call" | custom-call | tf_op jit(solution)/shard_map/project/pallas_call | solution.py:62
  11.4 3.1 %collective-permute-start.3 = (bf16[272,256]{1,0:T(8,128)(2,1)}, bf16[272,256]{1,0:T(8,128)(2,1)S(1)}, u32[]{:S(2)}, u32[]{:S(2)}) collective-permute-start(bf16[272,256]{1,0:T(8,128)(2,1)} %get-tuple-element.66), channel_id=1, source_target_pairs={{0,1},{1,0},{16,17},{17,16},{2,3},{3,2},{18,19},{19,18},{4,5},{5,4... | collective-permute-start | bytes 417800 | tf_op jit(solution)/shard_map/ppermute | solution.py:342
  34.7 3.2 %collective-permute-start.9 = (bf16[4,144,256]{2,1,0:T(8,128)(2,1)S(1)}, bf16[4,144,256]{2,1,0:T(8,128)(2,1)}, u32[]{:S(2)}, u32[]{:S(2)}) collective-permute-start(bf16[4,144,256]{2,1,0:T(8,128)(2,1)S(1)} %copy-done.4), channel_id=1, source_target_pairs={{0,128},{32,160},{64,192},{96,224},{128,0},{160,32},{192,64},{224,... | collective-permute-start | bytes 884744 | tf_op jit(solution)/shard_map/ppermute | solution.py:386
  38.0 4.3 %collective-permute-done = bf16[1168,128]{1,0:T(8,128)(2,1)S(1)} collective-permute-done((bf16[1168,128]{1,0:T(8,128)(2,1)S(1)}, bf16[1168,128]{1,0:T(8,128)(2,1)S(1)}, u32[]{:S(2)}, u32[]{:S(2)}) %collective-permute-start) | collective-permute-done | bytes 299040 | tf_op jit(solution)/shard_map/ppermute | solution.py:342
  44.6 6.7 %collective-permute-done.13.refs_8_ = bf16[4,128,256]{2,1,0:T(8,128)(2,1)} collective-permute-done((bf16[4,128,256]{2,1,0:T(8,128)(2,1)S(1)}, bf16[4,128,256]{2,1,0:T(8,128)(2,1)}, u32[]{:S(2)}, u32[]{:S(2)}) %collective-permute-start.13) | collective-permute-done | bytes 262176 | tf_op jit(solution)/shard_map/ppermute | solution.py:380
  54.3 4.1 %collective-permute-start.10 = (bf16[4,144,256]{2,1,0:T(8,128)(2,1)S(1)}, bf16[4,144,256]{2,1,0:T(8,128)(2,1)S(1)}, u32[]{:S(2)}, u32[]{:S(2)}) collective-permute-start(bf16[4,144,256]{2,1,0:T(8,128)(2,1)S(1)} %collective-permute-done.7.refs_18_.refs_16_), channel_id=1, source_target_pairs={{0,128},{32,160},{64,192},{96,224},{128,0},{160,32},{192,64},{224,... | collective-permute-start | bytes 884744 | tf_op jit(solution)/shard_map/ppermute | solution.py:386
  60.8 6.2 %collective-permute-done.11.refs_15_.refs_13_ = bf16[4,144,256]{2,1,0:T(8,128)(2,1)S(1)} collective-permute-done((bf16[4,144,256]{2,1,0:T(8,128)(2,1)S(1)}, bf16[4,144,256]{2,1,0:T(8,128)(2,1)S(1)}, u32[]{:S(2)}, u32[]{:S(2)}) %collective-permute-start.11) | collective-permute-done | bytes 294944 | tf_op jit(solution)/shard_map/ppermute | solution.py:386
  69.7 3.3 %collective-permute-done.12.refs_16_.refs_14_ = bf16[4,144,256]{2,1,0:T(8,128)(2,1)S(1)} collective-permute-done((bf16[4,144,256]{2,1,0:T(8,128)(2,1)S(1)}, bf16[4,144,256]{2,1,0:T(8,128)(2,1)S(1)}, u32[]{:S(2)}, u32[]{:S(2)}) %collective-permute-start.12) | collective-permute-done | bytes 294944 | tf_op jit(solution)/shard_map/ppermute | solution.py:386
  74.1 6.1 %attend_forward.2 = (bf16[4,144,256]{2,1,0:T(8,128)(2,1)}, bf16[4,144,256]{2,1,0:T(8,128)(2,1)}, bf16[4,144,256]{2,1,0:T(8,128)(2,1)}) custom-call(s32[4]{0:T(128)} %slice_reduce_fusion.refs_0_, s32[32]{0:T(128)} %get-tuple-element.134.refs_1_.refs_3_.refs_4_, s32[32]{0:T(128)} %get-tuple-element.133.refs_2_.refs_1_.refs_3_.refs_4_, ...), custom_call_target="tpu_custom_call" | custom-call | flops 17179869184 | bytes 1048576 | tf_op jit(solution)/shard_map/attend_forward/pallas_call | solution.py:274
  84.7 7.6 %collective-permute-start.17 = (bf16[8,128,256]{2,1,0:T(8,128)(2,1)}, bf16[8,128,256]{2,1,0:T(8,128)(2,1)}, u32[]{:S(2)}, u32[]{:S(2)}) collective-permute-start(bf16[8,128,256]{2,1,0:T(8,128)(2,1)} %pair.1.refs_9_), channel_id=1, source_target_pairs={{0,128},{32,160},{64,192},{96,224},{128,0},{160,32},{192,64},{224,... | collective-permute-start | bytes 1572872 | tf_op jit(solution)/shard_map/ppermute | solution.py:418
  92.3 14.1 %attend_forward.3 = bf16[32,144,256]{2,1,0:T(8,128)(2,1)} custom-call(s32[4]{0:T(128)} %slice_reduce_fusion.refs_0_, s32[32]{0:T(128)} %copy-done.26, s32[32]{0:T(128)} %get-tuple-element.133.refs_2_.refs_1_.refs_3_.refs_4_, s32[32]{0:T(128)} %copy-done.26, s32[32]{0:T(128)} %get-tuple-element.134.refs_1_.refs_3_.refs_4_, bf16[4,1168,128]{2,1,0:T(8,128)(2,1)} %copy-done, ...), custom_call_target="tpu_custom_call" | custom-call | flops 17179869184 | bytes 1048576 | tf_op jit(solution)/shard_map/attend_forward/pallas_call | solution.py:274
  106.4 8.4 %collective-permute-done.17.refs_9_ = bf16[8,128,256]{2,1,0:T(8,128)(2,1)} collective-permute-done((bf16[8,128,256]{2,1,0:T(8,128)(2,1)}, bf16[8,128,256]{2,1,0:T(8,128)(2,1)}, u32[]{:S(2)}, u32[]{:S(2)}) %collective-permute-start.17) | collective-permute-done | bytes 524320 | tf_op jit(solution)/shard_map/ppermute | solution.py:418
  115.7 20.8 %all-to-all-start = ((bf16[32,144,256]{2,1,0:T(8,128)(2,1)}), bf16[32,144,256]{2,1,0:T(8,128)(2,1)S(1)}, u32[]{:S(2)}, u32[]{:S(2)}) async-start(bf16[32,144,256]{2,1,0:T(8,128)(2,1)} %attend_forward.3), calls=%async_computation | async-start | bytes 4718592 | tf_op jit(solution)/shard_map/all_to_all | solution.py:431
  139.0 24.6 %all-gather.5.cloned.1.call-done.refs_10_ = bf16[32,144,256]{2,1,0:T(8,128)(2,1)} async-done(((bf16[4,144,256]{2,1,0:T(8,128)(2,1)}), bf16[32,144,256]{2,1,0:T(8,128)(2,1)}) %all-gather.5.cloned.1.call-update) | async-done | bytes 2359312 | tf_op jit(solution)/shard_map/all_gather | solution.py:417
  163.6 9.7 %attend_backward.2 = (bf16[4,144,256]{2,1,0:T(8,128)(2,1)}, bf16[4,144,256]{2,1,0:T(8,128)(2,1)}, bf16[4,144,256]{2,1,0:T(8,128)(2,1)}, bf16[4,144,256]{2,1,0:T(8,128)(2,1)}) custom-call(s32[4]{0:T(128)} %slice_reduce_fusion.refs_0_, s32[32]{0:T(128)} %get-tuple-element.133.refs_2_.refs_1_.refs_3_.refs_4_, s32[32]{0:T(128)} %copy-done.26, ...), custom_call_target="tpu_custom_call" | custom-call | flops 17179869184 | bytes 1048576 | tf_op jit(solution)/shard_map/attend_backward/pallas_call | solution.py:274
  173.3 25.6 %collective-permute-done.19.refs_0_ = bf16[4,144,256]{2,1,0:T(8,128)(2,1)S(1)} collective-permute-done((bf16[4,144,256]{2,1,0:T(8,128)(2,1)}, bf16[4,144,256]{2,1,0:T(8,128)(2,1)S(1)}, u32[]{:S(2)}, u32[]{:S(2)}) %collective-permute-start.19) | collective-permute-done | bytes 294944 | tf_op jit(solution)/shard_map/ppermute | solution.py:380
  202.4 4.2 %collective-permute-start.22 = (bf16[4,144,256]{2,1,0:T(8,128)(2,1)}, bf16[4,144,256]{2,1,0:T(8,128)(2,1)S(1)}, u32[]{:S(2)}, u32[]{:S(2)}) collective-permute-start(bf16[4,144,256]{2,1,0:T(8,128)(2,1)} %get-tuple-element.110), channel_id=1, source_target_pairs={{0,224},{32,192},{64,32},{96,0},{128,96},{160,64},{192,160},{224,1... | collective-permute-start | bytes 884744 | tf_op jit(solution)/shard_map/ppermute | solution.py:452
  206.6 3.4 %collective-permute-start.24 = (bf16[4,144,256]{2,1,0:T(8,128)(2,1)}, bf16[4,144,256]{2,1,0:T(8,128)(2,1)S(1)}, u32[]{:S(2)}, u32[]{:S(2)}) collective-permute-start(bf16[4,144,256]{2,1,0:T(8,128)(2,1)} %get-tuple-element.112), channel_id=1, source_target_pairs={{0,160},{32,128},{64,224},{96,192},{128,32},{160,0},{192,96},{224,... | collective-permute-start | bytes 884744 | tf_op jit(solution)/shard_map/ppermute | solution.py:452
  210.1 9.7 %attend_backward.3 = (bf16[4,144,256]{2,1,0:T(8,128)(2,1)}, bf16[4,144,256]{2,1,0:T(8,128)(2,1)}, bf16[4,144,256]{2,1,0:T(8,128)(2,1)}, bf16[4,144,256]{2,1,0:T(8,128)(2,1)}) custom-call(s32[4]{0:T(128)} %slice_reduce_fusion.refs_0_, s32[32]{0:T(128)} %get-tuple-element.133.refs_2_.refs_1_.refs_3_.refs_4_, s32[32]{0:T(128)} %copy-done.26, ...), custom_call_target="tpu_custom_call" | custom-call | flops 17179869184 | bytes 1048576 | tf_op jit(solution)/shard_map/attend_backward/pallas_call | solution.py:274
  219.8 8.1 %collective-permute-done.21.refs_3_ = bf16[4,144,256]{2,1,0:T(8,128)(2,1)S(1)} collective-permute-done((bf16[4,144,256]{2,1,0:T(8,128)(2,1)}, bf16[4,144,256]{2,1,0:T(8,128)(2,1)S(1)}, u32[]{:S(2)}, u32[]{:S(2)}) %collective-permute-start.21) | collective-permute-done | bytes 294944 | tf_op jit(solution)/shard_map/ppermute | solution.py:452
  233.0 6.6 %attend_self.1.refs_11_ = bf16[4,144,256]{2,1,0:T(8,128)(2,1)S(1)} custom-call(bf16[4,128,256]{2,1,0:T(8,128)(2,1)S(1)} %copy-done.3, bf16[4,144,256]{2,1,0:T(8,128)(2,1)S(1)} %copy-done.5, bf16[4,1168,128]{2,1,0:T(8,128)(2,1)S(1)} %copy-done.1, bf16[256,128]{1,0:T(8,128)(2,1)S(1)} %copy-done.7, f32[1,256]{1,0:T(1,128)S(1)} %copy-done.9), custom_call_target="tpu_custom_call" | custom-call | flops 8589934592 | bytes 1048576 | tf_op jit(solution)/shard_map/attend_self/pallas_call | solution.py:274
  246.2 5.6 %merge.1 = bf16[4,128,256]{2,1,0:T(8,128)(2,1)} custom-call(s32[1]{0:T(128)} %bitcast.1.place, bf16[8,4,144,256]{3,2,1,0:T(8,128)(2,1)} %bitcast.34, bf16[4,144,256]{2,1,0:T(8,128)(2,1)} %copy-done.12, bf16[4,144,256]{2,1,0:T(8,128)(2,1)} %get-tuple-element.114.refs_1_, bf16[4,144,256]{2,1,0:T(8,128)(2,1)} %copy-done.13, bf16[4,144,256]{2,1,0:T(8,128)(2,1)} %copy-done.14, ...), custom_call_target="tpu_custom_call" | custom-call | tf_op jit(solution)/shard_map/merge/pallas_call | solution.py:307
  251.8 3.4 %all-to-all-start.1 = ((bf16[4,128,256]{2,1,0:T(8,128)(2,1)}), bf16[4,128,256]{2,1,0:T(8,128)(2,1)S(1)}, u32[]{:S(2)}, u32[]{:S(2)}) async-start(bf16[4,128,256]{2,1,0:T(8,128)(2,1)} %merge.1), calls=%async_computation.1 | async-start | bytes 524288 | tf_op jit(solution)/shard_map/all_to_all | solution.py:457
  255.3 7.5 %all-to-all-done.1 = bf16[4,128,256]{2,1,0:T(8,128)(2,1)S(1)} async-done(((bf16[4,128,256]{2,1,0:T(8,128)(2,1)}), bf16[4,128,256]{2,1,0:T(8,128)(2,1)S(1)}, u32[]{:S(2)}, u32[]{:S(2)}) %all-to-all-start.1) | async-done | bytes 262176 | tf_op jit(solution)/shard_map/all_to_all | solution.py:457
  (150 shorter events, 55.3 us)
Async XLA Ops:
  6.5 76.5 %all-gather.3.cloned.1.call-start = ((), (), s32[]{:S(2)}) async-start(), calls=%async_computation.2 | async-start | bytes 2359296 | tf_op jit(solution)/shard_map/all_gather | solution.py:382
  24.1 139.5 %all-gather.5.cloned.1.call-start = ((), (), s32[]{:S(2)}) async-start(), calls=%async_computation.3 | async-start | bytes 2654208 | tf_op jit(solution)/shard_map/all_gather | solution.py:417
  26.9 15.4 %collective-permute-start = (bf16[1168,128]{1,0:T(8,128)(2,1)S(1)}, bf16[1168,128]{1,0:T(8,128)(2,1)S(1)}, u32[]{:S(2)}, u32[]{:S(2)}) collective-permute-start(bf16[1168,128]{1,0:T(8,128)(2,1)S(1)} %get-tuple-element.128), channel_id=1, source_target_pairs={{0,1},{1,0},{16,17},{17,16},{2,3},{3,2},{18,19},{19,18},{4,5},{5,4... | collective-permute-start | bytes 897032 | tf_op jit(solution)/shard_map/ppermute | solution.py:342
  29.7 28.8 %collective-permute-start.6 = (bf16[4,144,256]{2,1,0:T(8,128)(2,1)S(1)}, bf16[4,144,256]{2,1,0:T(8,128)(2,1)S(1)}, u32[]{:S(2)}, u32[]{:S(2)}) collective-permute-start(bf16[4,144,256]{2,1,0:T(8,128)(2,1)S(1)} %copy-done.4), channel_id=1, source_target_pairs={{0,64},{32,96},{64,128},{96,160},{128,192},{160,224},{192,0},{224,... | collective-permute-start | bytes 884744 | tf_op jit(solution)/shard_map/ppermute | solution.py:386
  31.3 22.2 %collective-permute-start.7 = (bf16[4,144,256]{2,1,0:T(8,128)(2,1)S(1)}, bf16[4,144,256]{2,1,0:T(8,128)(2,1)S(1)}, u32[]{:S(2)}, u32[]{:S(2)}) collective-permute-start(bf16[4,144,256]{2,1,0:T(8,128)(2,1)S(1)} %copy-done.4), channel_id=1, source_target_pairs={{0,32},{32,0},{64,96},{96,64},{128,160},{160,128},{192,224},{224,1... | collective-permute-start | bytes 884744 | tf_op jit(solution)/shard_map/ppermute | solution.py:383
  34.7 26.1 %collective-permute-start.9 = (bf16[4,144,256]{2,1,0:T(8,128)(2,1)S(1)}, bf16[4,144,256]{2,1,0:T(8,128)(2,1)}, u32[]{:S(2)}, u32[]{:S(2)}) collective-permute-start(bf16[4,144,256]{2,1,0:T(8,128)(2,1)S(1)} %copy-done.4), channel_id=1, source_target_pairs={{0,128},{32,160},{64,192},{96,224},{128,0},{160,32},{192,64},{224,... | collective-permute-start | bytes 884744 | tf_op jit(solution)/shard_map/ppermute | solution.py:386
  37.9 13.4 %collective-permute-start.13 = (bf16[4,128,256]{2,1,0:T(8,128)(2,1)S(1)}, bf16[4,128,256]{2,1,0:T(8,128)(2,1)}, u32[]{:S(2)}, u32[]{:S(2)}) collective-permute-start(bf16[4,128,256]{2,1,0:T(8,128)(2,1)S(1)} %copy-done.2), channel_id=1, source_target_pairs={{0,14},{2,0},{4,2},{6,4},{8,6},{10,8},{12,10},{14,12},{1,15},{3,1}... | collective-permute-start | bytes 786440 | tf_op jit(solution)/shard_map/ppermute | solution.py:380
  51.4 15.7 %collective-permute-start.11 = (bf16[4,144,256]{2,1,0:T(8,128)(2,1)S(1)}, bf16[4,144,256]{2,1,0:T(8,128)(2,1)S(1)}, u32[]{:S(2)}, u32[]{:S(2)}) collective-permute-start(bf16[4,144,256]{2,1,0:T(8,128)(2,1)S(1)} %copy-done.4), channel_id=1, source_target_pairs={{0,192},{32,224},{64,0},{96,32},{128,64},{160,96},{192,128},{224,1... | collective-permute-start | bytes 884744 | tf_op jit(solution)/shard_map/ppermute | solution.py:386
  53.5 16.3 %collective-permute-start.8 = (bf16[4,144,256]{2,1,0:T(8,128)(2,1)S(1)}, bf16[4,144,256]{2,1,0:T(8,128)(2,1)S(1)}, u32[]{:S(2)}, u32[]{:S(2)}) collective-permute-start(bf16[4,144,256]{2,1,0:T(8,128)(2,1)S(1)} %collective-permute-done.7.refs_18_.refs_16_), channel_id=1, source_target_pairs={{0,64},{32,96},{64,128},{96,160},{128,192},{160,224},{192,0},{224,... | collective-permute-start | bytes 884744 | tf_op jit(solution)/shard_map/ppermute | solution.py:386
  54.3 15.4 %collective-permute-start.10 = (bf16[4,144,256]{2,1,0:T(8,128)(2,1)S(1)}, bf16[4,144,256]{2,1,0:T(8,128)(2,1)S(1)}, u32[]{:S(2)}, u32[]{:S(2)}) collective-permute-start(bf16[4,144,256]{2,1,0:T(8,128)(2,1)S(1)} %collective-permute-done.7.refs_18_.refs_16_), channel_id=1, source_target_pairs={{0,128},{32,160},{64,192},{96,224},{128,0},{160,32},{192,64},{224,... | collective-permute-start | bytes 884744 | tf_op jit(solution)/shard_map/ppermute | solution.py:386
  58.5 14.6 %collective-permute-start.12 = (bf16[4,144,256]{2,1,0:T(8,128)(2,1)S(1)}, bf16[4,144,256]{2,1,0:T(8,128)(2,1)S(1)}, u32[]{:S(2)}, u32[]{:S(2)}) collective-permute-start(bf16[4,144,256]{2,1,0:T(8,128)(2,1)S(1)} %collective-permute-done.7.refs_18_.refs_16_), channel_id=1, source_target_pairs={{0,192},{32,224},{64,0},{96,32},{128,64},{160,96},{192,128},{224,1... | collective-permute-start | bytes 884744 | tf_op jit(solution)/shard_map/ppermute | solution.py:386
  83.1 23.3 %collective-permute-start.16 = (bf16[8,128,256]{2,1,0:T(8,128)(2,1)}, bf16[8,128,256]{2,1,0:T(8,128)(2,1)S(1)}, u32[]{:S(2)}, u32[]{:S(2)}) collective-permute-start(bf16[8,128,256]{2,1,0:T(8,128)(2,1)} %pair.1.refs_9_), channel_id=1, source_target_pairs={{0,64},{32,96},{64,128},{96,160},{128,192},{160,224},{192,0},{224,... | collective-permute-start | bytes 1572872 | tf_op jit(solution)/shard_map/ppermute | solution.py:418
  84.7 30.1 %collective-permute-start.17 = (bf16[8,128,256]{2,1,0:T(8,128)(2,1)}, bf16[8,128,256]{2,1,0:T(8,128)(2,1)}, u32[]{:S(2)}, u32[]{:S(2)}) collective-permute-start(bf16[8,128,256]{2,1,0:T(8,128)(2,1)} %pair.1.refs_9_), channel_id=1, source_target_pairs={{0,128},{32,160},{64,192},{96,224},{128,0},{160,32},{192,64},{224,... | collective-permute-start | bytes 1572872 | tf_op jit(solution)/shard_map/ppermute | solution.py:418
  92.3 22.5 %collective-permute-start.18 = (bf16[8,128,256]{2,1,0:T(8,128)(2,1)}, bf16[8,128,256]{2,1,0:T(8,128)(2,1)S(1)}, u32[]{:S(2)}, u32[]{:S(2)}) collective-permute-start(bf16[8,128,256]{2,1,0:T(8,128)(2,1)} %pair.1.refs_9_), channel_id=1, source_target_pairs={{0,192},{32,224},{64,0},{96,32},{128,64},{160,96},{192,128},{224,1... | collective-permute-start | bytes 1572872 | tf_op jit(solution)/shard_map/ppermute | solution.py:418
  115.7 124.7 %all-to-all-start = ((bf16[32,144,256]{2,1,0:T(8,128)(2,1)}), bf16[32,144,256]{2,1,0:T(8,128)(2,1)S(1)}, u32[]{:S(2)}, u32[]{:S(2)}) async-start(bf16[32,144,256]{2,1,0:T(8,128)(2,1)} %attend_forward.3), calls=%async_computation | async-start | bytes 4718592 | tf_op jit(solution)/shard_map/all_to_all | solution.py:431
  137.0 61.9 %collective-permute-start.19 = (bf16[4,144,256]{2,1,0:T(8,128)(2,1)}, bf16[4,144,256]{2,1,0:T(8,128)(2,1)S(1)}, u32[]{:S(2)}, u32[]{:S(2)}) collective-permute-start(bf16[4,144,256]{2,1,0:T(8,128)(2,1)} %get-tuple-element.96), channel_id=1, source_target_pairs={{0,2},{2,4},{4,6},{6,8},{8,10},{10,12},{12,14},{14,0},{1,3},{3,5},... | collective-permute-start | bytes 884744 | tf_op jit(solution)/shard_map/ppermute | solution.py:380
  138.5 61.1 %collective-permute-start.20 = (bf16[4,144,256]{2,1,0:T(8,128)(2,1)}, bf16[4,144,256]{2,1,0:T(8,128)(2,1)S(1)}, u32[]{:S(2)}, u32[]{:S(2)}) collective-permute-start(bf16[4,144,256]{2,1,0:T(8,128)(2,1)} %get-tuple-element.98), channel_id=1, source_target_pairs={{0,14},{2,0},{4,2},{6,4},{8,6},{10,8},{12,10},{14,12},{1,15},{3,1}... | collective-permute-start | bytes 884744 | tf_op jit(solution)/shard_map/ppermute | solution.py:380
  199.6 28.3 %collective-permute-start.21 = (bf16[4,144,256]{2,1,0:T(8,128)(2,1)}, bf16[4,144,256]{2,1,0:T(8,128)(2,1)S(1)}, u32[]{:S(2)}, u32[]{:S(2)}) collective-permute-start(bf16[4,144,256]{2,1,0:T(8,128)(2,1)} %get-tuple-element.109), channel_id=1, source_target_pairs={{0,192},{32,224},{64,0},{96,32},{128,64},{160,96},{192,128},{224,1... | collective-permute-start | bytes 884744 | tf_op jit(solution)/shard_map/ppermute | solution.py:452
  202.4 25.5 %collective-permute-start.22 = (bf16[4,144,256]{2,1,0:T(8,128)(2,1)}, bf16[4,144,256]{2,1,0:T(8,128)(2,1)S(1)}, u32[]{:S(2)}, u32[]{:S(2)}) collective-permute-start(bf16[4,144,256]{2,1,0:T(8,128)(2,1)} %get-tuple-element.110), channel_id=1, source_target_pairs={{0,224},{32,192},{64,32},{96,0},{128,96},{160,64},{192,160},{224,1... | collective-permute-start | bytes 884744 | tf_op jit(solution)/shard_map/ppermute | solution.py:452
  206.6 21.3 %collective-permute-start.23 = (bf16[4,144,256]{2,1,0:T(8,128)(2,1)}, bf16[4,144,256]{2,1,0:T(8,128)(2,1)S(1)}, u32[]{:S(2)}, u32[]{:S(2)}) collective-permute-start(bf16[4,144,256]{2,1,0:T(8,128)(2,1)} %get-tuple-element.111), channel_id=1, source_target_pairs={{0,128},{32,160},{64,192},{96,224},{128,0},{160,32},{192,64},{224,... | collective-permute-start | bytes 884744 | tf_op jit(solution)/shard_map/ppermute | solution.py:452
  206.6 21.3 %collective-permute-start.24 = (bf16[4,144,256]{2,1,0:T(8,128)(2,1)}, bf16[4,144,256]{2,1,0:T(8,128)(2,1)S(1)}, u32[]{:S(2)}, u32[]{:S(2)}) collective-permute-start(bf16[4,144,256]{2,1,0:T(8,128)(2,1)} %get-tuple-element.112), channel_id=1, source_target_pairs={{0,160},{32,128},{64,224},{96,192},{128,32},{160,0},{192,96},{224,... | collective-permute-start | bytes 884744 | tf_op jit(solution)/shard_map/ppermute | solution.py:452
  228.0 14.3 %collective-permute-start.25 = (bf16[4,144,256]{2,1,0:T(8,128)(2,1)}, bf16[4,144,256]{2,1,0:T(8,128)(2,1)S(1)}, u32[]{:S(2)}, u32[]{:S(2)}) collective-permute-start(bf16[4,144,256]{2,1,0:T(8,128)(2,1)} %get-tuple-element.120), channel_id=1, source_target_pairs={{0,64},{32,96},{64,128},{96,160},{128,192},{160,224},{192,0},{224,... | collective-permute-start | bytes 884744 | tf_op jit(solution)/shard_map/ppermute | solution.py:452
  229.5 14.1 %collective-permute-start.26 = (bf16[4,144,256]{2,1,0:T(8,128)(2,1)}, bf16[4,144,256]{2,1,0:T(8,128)(2,1)S(1)}, u32[]{:S(2)}, u32[]{:S(2)}) collective-permute-start(bf16[4,144,256]{2,1,0:T(8,128)(2,1)} %get-tuple-element.121), channel_id=1, source_target_pairs={{0,96},{32,64},{64,160},{96,128},{128,224},{160,192},{192,32},{224... | collective-permute-start | bytes 884744 | tf_op jit(solution)/shard_map/ppermute | solution.py:452
  232.1 14.1 %collective-permute-start.27 = (bf16[4,144,256]{2,1,0:T(8,128)(2,1)}, bf16[4,144,256]{2,1,0:T(8,128)(2,1)}, u32[]{:S(2)}, u32[]{:S(2)}) collective-permute-start(bf16[4,144,256]{2,1,0:T(8,128)(2,1)} %get-tuple-element.123), channel_id=1, source_target_pairs={{0,32},{32,0},{64,96},{96,64},{128,160},{160,128},{192,224},{224,1... | collective-permute-start | bytes 884744 | tf_op jit(solution)/shard_map/ppermute | solution.py:452
  (45 other events, 536.8 us)
Sparse Core Ops, SparseCore 0:
  24.3 45.5 all-gather.2
  83.2 80.4 all-gather.4
